TPU v7x, 32 devices: a whole 2x2x4 slice. The times are simulated.
32 devices in a mesh: ctx: 4 (over x, core), mp: 8 (over z, y).
Axes of the slice: x: 2, y: 2, z: 4, core: 2. Of those that a mesh axis runs over, the one named last changes fastest.
Arguments:
- queries: bfloat16 [4096, 4096], P('ctx', 'mp'), may hold values from -320 to 320
- keys_values: bfloat16 [4096, 2048], P('ctx', 'mp'), may hold values from -40 to 40
- query_taps: float32 [4, 4096], P(None, 'mp'), may hold values from -2.5 to 2.5
- pair_taps: float32 [4, 2048], P(None, 'mp'), may hold values from -2.5 to 2.5
- out_gain: float32 [4096], P('mp'), may hold values from 0.1 to 1.9
Outputs:
- head_outputs: bfloat16 [4096, 4096], P('ctx', 'mp')
All inputs are finite; a program needn't handle non-finite values.
Results may differ from a plain program's by a relative error of at most 0.012.
The roundings to bfloat16 on the way count: a program that leaves them out, or rounds other values in their place, can miss the bound.
Values may be sent and summed in bfloat16 or wider, within the bound.
A program may use at most 64 MiB of HBM per device.

v0:
```python
import math

import jax
import jax.numpy as jnp
from jax import lax
from jax.sharding import PartitionSpec as P

HEAD_CHANNELS = 128
TAPS = 4
TRANSFORM_BLOCK = 128
KEEP = 16


NEGATIVE = -1e30
EPSILON = 1e-06


def shifted(value, axis, steps):
    count = lax.axis_size(axis)
    leading, last = (max(0, -steps), min(count, count - steps))
    return lax.ppermute(value, axis, [(source, source + steps) for source in range(leading, last)])


def for_sending(value):
    return jax.tree.map(lambda a: a.astype(jnp.bfloat16) if a.dtype == jnp.float32 else a, value)


def from_partner(block, axis, apart):
    count = lax.axis_size(axis)
    route = []
    for low in range(count):
        high = low | 1 << apart
        if high != low and high < count:
            route += [(low, high), (high, low)]
    return lax.ppermute(block, axis, route)


def dct_table():
    frequency = jnp.arange(KEEP, dtype=jnp.float32)[:, None]
    offset = jnp.arange(TRANSFORM_BLOCK, dtype=jnp.float32)[None, :]
    table = jnp.cos(math.pi * (offset + 0.5) * frequency / TRANSFORM_BLOCK) * math.sqrt(
        2.0 / TRANSFORM_BLOCK
    )
    table = jnp.where(frequency == 0.0, table * math.sqrt(0.5), table)
    return table.astype(jnp.bfloat16)


def compress(values):
    blocks = values.reshape(values.shape[0] // TRANSFORM_BLOCK, TRANSFORM_BLOCK, values.shape[1])
    packed = jnp.einsum("jt,btc->bjc", dct_table(), blocks, preferred_element_type=jnp.float32)
    return packed.astype(jnp.bfloat16).reshape(-1, values.shape[1])


def causal_conv(history, values, weights):
    lead = weights.shape[0] - 1
    padded = jnp.concatenate([history, values], 0)
    length = values.shape[0]
    total = weights[0] * values.astype(jnp.float32)
    for shift in range(1, weights.shape[0]):
        total = total + weights[shift] * padded[lead - shift : lead - shift + length].astype(
            jnp.float32
        )
    return total.astype(jnp.bfloat16)


def local_state(query_heads, pairs, score_scale):
    entry_count = query_heads.shape[0] // TRANSFORM_BLOCK
    heads = query_heads.shape[1]
    scores = (
        jnp.einsum(
            "uxwi,umi->uxwm",
            query_heads.reshape(entry_count, TRANSFORM_BLOCK, heads, HEAD_CHANNELS),
            pairs[:, :HEAD_CHANNELS].reshape(entry_count, TRANSFORM_BLOCK, HEAD_CHANNELS),
            preferred_element_type=jnp.float32,
        )
        * score_scale
    )
    causal = (
        jnp.arange(TRANSFORM_BLOCK)[:, None, None] >= jnp.arange(TRANSFORM_BLOCK)[None, None, :]
    )
    scores = jnp.where(causal, scores, NEGATIVE)
    top = jnp.max(scores, -1)
    weights = jnp.where(causal, jnp.exp(scores - top[..., None]), 0.0)
    total = jnp.sum(weights, -1)
    summed = jnp.einsum(
        "cevo,coa->ceva",
        weights.astype(jnp.bfloat16),
        pairs[:, HEAD_CHANNELS:].reshape(entry_count, TRANSFORM_BLOCK, HEAD_CHANNELS),
        preferred_element_type=jnp.float32,
    )
    rows = entry_count * TRANSFORM_BLOCK
    return (
        top.reshape(rows, heads),
        total.reshape(rows, heads),
        summed.reshape(rows, heads, HEAD_CHANNELS),
    )


def attend(state, query_heads, query_blocks, keys, key_blocks, score_scale):
    top, total, summed = state
    entry_count = query_heads.shape[0]
    size = 512
    tops, totals, sums = ([], [], [])
    for begin in range(0, entry_count, size):
        part = query_heads[begin : begin + size]
        scores = (
            jnp.einsum(
                "qhd,kd->qhk", part, keys[:, :HEAD_CHANNELS], preferred_element_type=jnp.float32
            )
            * score_scale
        )
        seen = key_blocks[None, None, :] < query_blocks[begin : begin + size, None, None]
        scores = jnp.where(seen, scores, NEGATIVE)
        old_top = top[begin : begin + size]
        new_top = jnp.maximum(old_top, jnp.max(scores, -1))
        weights = jnp.where(seen, jnp.exp(scores - new_top[..., None]), 0.0)
        rescale = jnp.exp(old_top - new_top)
        totals.append(rescale * total[begin : begin + size] + jnp.sum(weights, -1))
        sums.append(
            rescale[..., None] * summed[begin : begin + size]
            + jnp.einsum(
                "qhk,kd->qhd",
                weights.astype(jnp.bfloat16),
                keys[:, HEAD_CHANNELS:],
                preferred_element_type=jnp.float32,
            )
        )
        tops.append(new_top)
    return (jnp.concatenate(tops, 0), jnp.concatenate(totals, 0), jnp.concatenate(sums, 0))


def per_device(queries, keys_values, query_taps, pair_taps, out_gain):
    rows = queries.shape[0]
    span_rows = rows // 2
    per_span = span_rows // TRANSFORM_BLOCK
    shards = lax.axis_size("ctx")
    place = lax.axis_index("ctx")
    member = lax.axis_index("mp")
    score_scale = 1.0 / math.sqrt(HEAD_CHANNELS)
    tail = TAPS - 1
    columns = queries.shape[1]
    first_tail = jnp.concatenate(
        [queries[span_rows - tail : span_rows], keys_values[span_rows - tail : span_rows]], 1
    )
    second_tail = jnp.concatenate([queries[rows - tail :], keys_values[rows - tail :]], 1)
    from_lower = shifted(first_tail, "ctx", 1)
    from_upper = shifted(second_tail, "ctx", -1)
    before_second = jnp.where(place == shards - 1, first_tail, from_upper)
    query_conv = jnp.concatenate(
        [
            causal_conv(from_lower[:, :columns], queries[:span_rows], query_taps),
            causal_conv(before_second[:, :columns], queries[span_rows:], query_taps),
        ],
        0,
    )
    pair_conv = jnp.concatenate(
        [
            causal_conv(from_lower[:, columns:], keys_values[:span_rows], pair_taps),
            causal_conv(before_second[:, columns:], keys_values[span_rows:], pair_taps),
        ],
        0,
    )
    width = keys_values.shape[1]
    rounds = (2 * HEAD_CHANNELS // width).bit_length() - 1

    def join(mine, other, bit):
        lower = member // 2**bit % 2 == 0
        return jnp.where(
            lower, jnp.concatenate([mine, other], 1), jnp.concatenate([other, mine], 1)
        )

    pairs = pair_conv
    packed = compress(pair_conv)
    for bit in range(rounds):
        other = from_partner(for_sending(jnp.concatenate([pairs, packed], 0)), "mp", bit)
        pairs = join(pairs, other[:rows], bit)
        packed = join(packed, other[rows:], bit)
    heads_here = columns // HEAD_CHANNELS
    query_heads = query_conv.reshape(rows, heads_here, HEAD_CHANNELS)
    own_rows = jnp.arange(rows)
    own_span = jnp.where(own_rows < span_rows, place, 2 * shards - 1 - place)
    query_blocks = own_span * per_span + own_rows % span_rows // TRANSFORM_BLOCK
    state = local_state(query_heads, pairs, score_scale)
    shard_rows = rows * KEEP // TRANSFORM_BLOCK
    half_rows = shard_rows // 2
    piece = lax.all_gather(packed, "ctx", axis=0, tiled=True)
    positions = jnp.arange(piece.shape[0])
    owner = positions // shard_rows
    within = positions % shard_rows
    span_index = jnp.where(within < half_rows, owner, 2 * shards - 1 - owner)
    key_blocks = span_index * per_span + within % half_rows // KEEP
    state = attend(state, query_heads, query_blocks, piece, key_blocks, score_scale)
    top, total, summed = state
    attended = summed / total[..., None]
    normed = attended * lax.rsqrt(jnp.mean(attended * attended, -1, keepdims=True) + EPSILON)
    return (normed.reshape(rows, columns) * out_gain).astype(jnp.bfloat16)


def solution(mesh):
    in_specs = (P("ctx", "mp"), P("ctx", "mp"), P(None, "mp"), P(None, "mp"), P("mp"))
    out_specs = P("ctx", "mp")
    return jax.shard_map(
        per_device, mesh=mesh, in_specs=in_specs, out_specs=out_specs, check_vma=False
    )
```

profile of v0, /device:TPU:0, one launch (start us, length us, event | category | flops | bytes accessed | tf_op | source)
XLA Modules:
  0.0 45.2 jit_solution(12742909706655654891)
XLA Ops:
  0.0 0.7 %fusion.98 = (bf16[3,256]{1,0:T(4,128)(2,1)S(1)}, bf16[3,256]{1,0:T(4,128)(2,1)S(1)}) fusion(bf16[1024,256]{1,0:T(8,128)(2,1)} %param.6), kind=kLoop, calls=%fused_computation.162 | loop fusion | bytes 6144 | tf_op jit(solution)/shard_map/slice | solution.py:143
  0.7 0.7 %fusion.96 = (bf16[3,512]{1,0:T(4,128)(2,1)S(1)}, bf16[3,512]{1,0:T(4,128)(2,1)S(1)}) fusion(bf16[1024,512]{1,0:T(8,128)(2,1)} %param.5), kind=kLoop, calls=%fused_computation.160 | loop fusion | bytes 12288 | tf_op jit(solution)/shard_map/slice | solution.py:143
  1.5 1.3 %collective-permute-start.1 = (bf16[3,768]{1,0:T(4,128)(2,1)S(1)}, bf16[3,768]{1,0:T(4,128)(2,1)S(1)}, u32[]{:S(2)}, u32[]{:S(2)}) collective-permute-start(bf16[3,768]{1,0:T(4,128)(2,1)S(1)} %pad_maximum_fusion.8), channel_id=1, source_target_pairs={{8,0},{16,8},{24,16},{9,1},{17,9},{25,17},{10,2},{18,10},{26,18},{... | collective-permute-start | bytes 13832 | tf_op jit(solution)/shard_map/ppermute | solution.py:21
  2.8 1.1 %fusion.97 = (bf16[512,256]{1,0:T(8,128)(2,1)S(1)}, bf16[512,256]{1,0:T(8,128)(2,1)S(1)}) fusion(bf16[1024,256]{1,0:T(8,128)(2,1)} %param.6), kind=kLoop, calls=%fused_computation.161 | loop fusion | bytes 1048576 | tf_op jit(solution)/shard_map/slice | solution.py:158
  3.9 1.3 %fusion.95 = (bf16[512,512]{1,0:T(8,128)(2,1)S(1)}, bf16[512,512]{1,0:T(8,128)(2,1)S(1)}) fusion(bf16[1024,512]{1,0:T(8,128)(2,1)} %param.5), kind=kLoop, calls=%fused_computation.159 | loop fusion | bytes 2097152 | tf_op jit(solution)/shard_map/slice | solution.py:151
  5.2 1.1 %broadcast_compare_fusion.1 = (pred[512,512]{0,1:T(8,128)(4,1)S(1)}, pred[512,512]{0,1:T(8,128)(4,1)}) fusion(s32[512]{0:T(512)S(1)} %get-tuple-element.33, s32[512]{0:T(512)S(1)} %fusion.75, s32[512]{0:T(512)S(1)} %get-tuple-element.34), kind=kLoop, calls=%fused_computation.62 | loop fusion | flops 524288 | bytes 530432 | tf_op jit(solution)/shard_map/lt | solution.py:112
  6.3 3.3 %collective-permute-start = (bf16[3,768]{1,0:T(4,128)(2,1)S(1)}, bf16[3,768]{1,0:T(4,128)(2,1)S(1)}, u32[]{:S(2)}, u32[]{:S(2)}) collective-permute-start(bf16[3,768]{1,0:T(4,128)(2,1)S(1)} %get-tuple-element.31), channel_id=1, source_target_pairs={{0,8},{8,16},{16,24},{1,9},{9,17},{17,25},{2,10},{10,18},{18,26},{... | collective-permute-start | bytes 13832 | tf_op jit(solution)/shard_map/ppermute | solution.py:21
  9.7 0.8 %collective-permute-done = bf16[3,768]{1,0:T(4,128)(2,1)S(1)} collective-permute-done((bf16[3,768]{1,0:T(4,128)(2,1)S(1)}, bf16[3,768]{1,0:T(4,128)(2,1)S(1)}, u32[]{:S(2)}, u32[]{:S(2)}) %collective-permute-start) | collective-permute-done | bytes 4640 | tf_op jit(solution)/shard_map/ppermute | solution.py:21
  10.5 0.5 %add_convert_fusion.3 = (bf16[512,256]{1,0:T(8,128)(2,1)S(1)}, bf16[512,256]{1,0:T(8,128)(2,1)S(1)}) fusion(bf16[512,256]{1,0:T(8,128)(2,1)S(1)} %get-tuple-element.17, bf16[3,256]{1,0:T(4,128)(2,1)S(1)} %slice.230, f32[256]{0:T(256)S(1)} %bitcast.113, f32[256]{0:T(256)S(1)} %bitcast.114, f32[256]{0:T(256)S(1)} %bitcast.112, f32[256]{0:T(256)S(1)} %bitcast.111, ...), kind=kLoop, calls=%fused_computation.64 | loop fusion | flops 5505024 | bytes 1055744 | tf_op jit(solution)/shard_map/convert_element_type | solution.py:63
  11.0 0.8 %fusion.49 = (bf16[1024,128]{1,0:T(8,128)(2,1)}, bf16[1024,128]{1,0:T(8,128)(2,1)}) fusion(bf16[512,256]{1,0:T(8,128)(2,1)S(1)} %get-tuple-element.35, bf16[512,256]{1,0:T(8,128)(2,1)S(1)} %get-tuple-element.36), kind=kLoop, calls=%fused_computation.74 | loop fusion | flops 1048576 | bytes 1048576 | tf_op jit(solution)/shard_map/concatenate | solution.py:156
  11.9 0.2 convolution_convert_fusion
  12.1 9.1 %all_gather.3 = bf16[512,256]{1,0:T(8,128)(2,1)} all-gather(bf16[128,256]{1,0:T(8,128)(2,1)S(1)} %bitcast.105), channel_id=1, replica_groups=mesh['ctx'=4,'mp'=8] {'ctx'}, dimensions={0}, use_global_device_ids=true | all-gather | bytes 327680 | tf_op jit(solution)/shard_map/all_gather | solution.py:186
  21.2 1.0 %add_convert_fusion.1 = (bf16[512,512]{1,0:T(8,128)(2,1)S(1)}, bf16[512,512]{1,0:T(8,128)(2,1)S(1)}) fusion(bf16[512,512]{1,0:T(8,128)(2,1)S(1)} %get-tuple-element.11, bf16[3,512]{1,0:T(4,128)(2,1)S(1)} %slice.220, f32[512]{0:T(512)S(1)} %bitcast.109, f32[512]{0:T(512)S(1)} %bitcast.110, f32[512]{0:T(512)S(1)} %bitcast.108, f32[512]{0:T(512)S(1)} %bitcast.107, ...), kind=kLoop, calls=%fused_computation.38 | loop fusion | flops 11010048 | bytes 2111488 | tf_op jit(solution)/shard_map/convert_element_type | solution.py:63
  22.3 0.3 reshape.215
  22.6 1.5 %fusion.16 = (f32[8,128,4]{1,2,0:T(4,128)S(1)}, f32[8,128,4,128]{1,3,2,0:T(8,128)S(1)}) fusion(pred[128,128]{0,1:T(8,128)(4,1)S(1)} %iota_compare_fusion, bf16[8,128,128,1]{2,1,3,0:T(8,128)(2,1)} %bitcast.106, bf16[8,128,4,128]{3,2,1,0:T(4,128)(2,1)S(1)} %reshape.215), kind=kOutput, calls=%fused_computation.23 | convolution fusion | flops 135786496 | bytes 3440640 | tf_op jit(solution)/shard_map/uxwi,umi->uxwm/dot_general | solution.py:70
  24.0 0.6 %fusion.17 = f32[8,128,4]{1,2,0:T(4,128)S(1)} fusion(f32[8,128,4,128]{1,3,2,0:T(8,128)S(1)} %get-tuple-element.44, f32[8,128,4]{1,2,0:T(4,128)S(1)} %get-tuple-element.43, pred[128,128]{0,1:T(8,128)(4,1)S(1)} %iota_compare_fusion), kind=kLoop, calls=%fused_computation.24 | loop fusion | flops 2617344 | bytes 2146304 | tf_op jit(solution)/shard_map/reduce_sum | solution.py:84
  24.6 0.7 %fusion.25 = f32[8,128,4,128]{3,1,2,0:T(8,128)S(1)} fusion(bf16[8,128,128,1]{2,1,3,0:T(8,128)(2,1)S(1)} %bitcast.104, f32[8,128,4,128]{1,3,2,0:T(8,128)S(1)} %get-tuple-element.44, f32[8,128,4]{1,2,0:T(4,128)S(1)} %get-tuple-element.43, pred[128,128]{0,1:T(8,128)(4,1)S(1)} %iota_compare_fusion), kind=kOutput, calls=%fused_computation.29 | convolution fusion | flops 136839168 | bytes 4489216 | tf_op jit(solution)/shard_map/cevo,coa->ceva/dot_general | solution.py:85
  25.7 1.3 %copy.37 = f32[512,4,128]{0,2,1:T(8,128)} copy(f32[512,4,128]{2,0,1:T(8,128)S(1)} %bitcast.101) | data formatting | bytes 2097152 | tf_op jit(solution)/shard_map/slice | solution.py:120
  27.1 1.3 %copy.42 = f32[512,4,128]{0,2,1:T(8,128)} copy(f32[512,4,128]{2,0,1:T(8,128)S(1)} %bitcast.102) | data formatting | bytes 2097152 | tf_op jit(solution)/shard_map/slice | solution.py:120
  28.4 0.9 %fusion = (f32[512,4]{0,1:T(4,128)S(1)}, f32[512,4,512]{0,2,1:T(8,128)S(1)}) fusion(pred[512,512]{0,1:T(8,128)(4,1)S(1)} %get-tuple-element.41, bf16[512,256]{1,0:T(8,128)(2,1)S(1)} %copy-done.5, bf16[512,512]{1,0:T(8,128)(2,1)S(1)} %get-tuple-element.25), kind=kOutput, calls=%fused_computation.4 | convolution fusion | flops 271579136 | bytes 5120000 | tf_op jit(solution)/shard_map/qhd,kd->qhk/dot_general | solution.py:107
  29.4 0.9 %fusion.1 = (f32[512,4]{0,1:T(4,128)S(1)}, f32[512,4,512]{0,2,1:T(8,128)S(1)}) fusion(pred[512,512]{0,1:T(8,128)(4,1)S(1)} %copy-done.1, bf16[512,256]{1,0:T(8,128)(2,1)S(1)} %copy-done.5, bf16[512,512]{1,0:T(8,128)(2,1)S(1)} %get-tuple-element.26), kind=kOutput, calls=%fused_computation.5 | convolution fusion | flops 271579136 | bytes 5120000 | tf_op jit(solution)/shard_map/qhd,kd->qhk/dot_general | solution.py:107
  30.3 2.1 %fusion.2 = (f32[512,4]{0,1:T(4,128)S(1)}, f32[512,4]{0,1:T(4,128)S(1)}) fusion(f32[512,4,512]{0,2,1:T(8,128)S(1)} %get-tuple-element.46, f32[512,4]{0,1:T(4,128)S(1)} %get-tuple-element.23, pred[512,512]{0,1:T(8,128)(4,1)S(1)} %get-tuple-element.41, f32[512,4]{0,1:T(4,128)S(1)} %get-tuple-element.24, f32[512,4,512]{0,2,1:T(8,128)S(1)} %get-tuple-element.48, ...), kind=kLoop, calls=%fused_computation.6 | loop fusion | flops 10481664 | bytes 8945664 | tf_op jit(solution)/shard_map/reduce_sum | solution.py:118
  32.4 1.2 %fusion.22 = f32[512,4,128]{0,2,1:T(8,128)S(1)} fusion(f32[512,4,512]{0,2,1:T(8,128)S(1)} %get-tuple-element.48, f32[512,4]{0,1:T(4,128)S(1)} %get-tuple-element.24, pred[512,512]{0,1:T(8,128)(4,1)S(1)} %copy-done.1, f32[512,4,128]{0,2,1:T(8,128)S(1)} %copy-done.3, f32[512,4]{0,1:T(4,128)S(1)} %get-tuple-element.22, bf16[512,256]{1,0:T(8,128)(2,1)S(1)} %copy-done.6), kind=kOutput, calls=%fused_computation.27 | convolution fusion | flops 274202624 | bytes 6701056 | tf_op jit(solution)/shard_map/qhk,kd->qhd/dot_general | solution.py:121
  33.7 1.2 %fusion.19 = f32[512,4,128]{0,2,1:T(8,128)S(1)} fusion(f32[512,4,512]{0,2,1:T(8,128)S(1)} %get-tuple-element.46, f32[512,4]{0,1:T(4,128)S(1)} %get-tuple-element.23, pred[512,512]{0,1:T(8,128)(4,1)S(1)} %get-tuple-element.41, f32[512,4,128]{0,2,1:T(8,128)S(1)} %copy-done.2, f32[512,4]{0,1:T(4,128)S(1)} %get-tuple-element.6, bf16[512,256]{1,0:T(8,128)(2,1)S(1)} %copy-done.6), kind=kOutput, calls=%fused_computation.26 | convolution fusion | flops 274202624 | bytes 6701056 | tf_op jit(solution)/shard_map/qhk,kd->qhd/dot_general | solution.py:121
  34.9 0.3 fusion.13
  35.2 1.0 %copy.48 = f32[1024,4]{1,0:T(8,128)} copy(f32[1024,4]{0,1:T(4,128)S(1)} %add_rsqrt_fusion) | data formatting | bytes 32768 | tf_op jit(solution)/shard_map/rsqrt | solution.py:195
  36.2 0.3 copy.45
  36.5 1.3 %copy.46 = f32[512,512]{1,0:T(8,128)} copy(f32[512,512]{0,1:T(8,128)S(1)} %bitcast.99) | data formatting | bytes 2097152 | tf_op jit(solution)/shard_map/concatenate | solution.py:129
  37.9 0.2 div.72
  38.1 1.9 %copy.47 = f32[1024,512]{1,0:T(8,128)} copy(f32[1024,512]{0,1:T(8,128)S(1)} %bitcast.98) | data formatting | bytes 4194304 | tf_op jit(solution)/shard_map/div | solution.py:194
  40.0 2.3 %mul.294 = f32[1024,4,128]{2,1,0:T(4,128)S(1)} broadcast(f32[1024,4]{1,0:T(8,128)} %copy.48), dimensions={0,1} | broadcast | bytes 2113536 | tf_op jit(solution)/shard_map/mul | solution.py:195
  42.3 2.9 %fusion.7 = bf16[1024,512]{1,0:T(8,128)(2,1)} fusion(f32[128,8,4,128]{3,2,1,0:T(4,128)S(1)} %bitcast.97, f32[1024,512]{1,0:T(8,128)S(1)} %copy-done, f32[512,512]{1,0:T(8,128)} %copy.46, f32[512,512]{1,0:T(8,128)S(1)} %copy.45, f32[512]{0:T(512)S(1)} %copy-done.9), kind=kLoop, calls=%fused_computation.12 | loop fusion | flops 2621440 | bytes 7342080 | tf_op jit(solution)/shard_map/convert_element_type | solution.py:196
  (44 shorter events, 0.8 us)
Async XLA Ops:
  0.0 5.2 %copy-start.8 = (f32[4,256]{1,0:T(4,128)S(1)}, f32[4,256]{1,0:T(4,128)}, u32[]{:S(2)}) copy-start(f32[4,256]{1,0:T(4,128)} %param.8) | copy-start | bytes 12292
  0.0 5.2 %copy-start.7 = (f32[4,512]{1,0:T(4,128)S(1)}, f32[4,512]{1,0:T(4,128)}, u32[]{:S(2)}) copy-start(f32[4,512]{1,0:T(4,128)} %param.7) | copy-start | bytes 24580
  1.5 4.9 %collective-permute-start.1 = (bf16[3,768]{1,0:T(4,128)(2,1)S(1)}, bf16[3,768]{1,0:T(4,128)(2,1)S(1)}, u32[]{:S(2)}, u32[]{:S(2)}) collective-permute-start(bf16[3,768]{1,0:T(4,128)(2,1)S(1)} %pad_maximum_fusion.8), channel_id=1, source_target_pairs={{8,0},{16,8},{24,16},{9,1},{17,9},{25,17},{10,2},{18,10},{26,18},{... | collective-permute-start | bytes 13832 | tf_op jit(solution)/shard_map/ppermute | solution.py:21
  6.3 4.1 %collective-permute-start = (bf16[3,768]{1,0:T(4,128)(2,1)S(1)}, bf16[3,768]{1,0:T(4,128)(2,1)S(1)}, u32[]{:S(2)}, u32[]{:S(2)}) collective-permute-start(bf16[3,768]{1,0:T(4,128)(2,1)S(1)} %get-tuple-element.31), channel_id=1, source_target_pairs={{0,8},{8,16},{16,24},{1,9},{9,17},{17,25},{2,10},{10,18},{18,26},{... | collective-permute-start | bytes 13832 | tf_op jit(solution)/shard_map/ppermute | solution.py:21
  22.6 2.1 %copy-start.4 = (bf16[1024,128]{1,0:T(8,128)(2,1)S(1)}, bf16[1024,128]{1,0:T(8,128)(2,1)}, u32[]{:S(2)}) copy-start(bf16[1024,128]{1,0:T(8,128)(2,1)} %get-tuple-element.15) | copy-start | bytes 786436
  27.1 1.3 %copy-start.5 = (bf16[512,256]{1,0:T(8,128)(2,1)S(1)}, bf16[512,256]{1,0:T(8,128)(2,1)}, u32[]{:S(2)}) copy-start(bf16[512,256]{1,0:T(8,128)(2,1)} %all_gather.3) | copy-start | bytes 786436
  28.4 1.0 %copy-start.1 = (pred[512,512]{0,1:T(8,128)(4,1)S(1)}, pred[512,512]{0,1:T(8,128)(4,1)}, u32[]{:S(2)}) copy-start(pred[512,512]{0,1:T(8,128)(4,1)} %get-tuple-element.42) | copy-start | bytes 786436
  30.3 2.2 %copy-start.3 = (f32[512,4,128]{0,2,1:T(8,128)S(1)}, f32[512,4,128]{0,2,1:T(8,128)}, u32[]{:S(2)}) copy-start(f32[512,4,128]{0,2,1:T(8,128)} %copy.42) | copy-start | bytes 3145732
  30.3 2.2 %copy-start.6 = (bf16[512,256]{1,0:T(8,128)(2,1)S(1)}, bf16[512,256]{1,0:T(8,128)(2,1)}, u32[]{:S(2)}) copy-start(bf16[512,256]{1,0:T(8,128)(2,1)} %all_gather.3) | copy-start | bytes 786436
  32.4 1.2 %copy-start.2 = (f32[512,4,128]{0,2,1:T(8,128)S(1)}, f32[512,4,128]{0,2,1:T(8,128)}, u32[]{:S(2)}) copy-start(f32[512,4,128]{0,2,1:T(8,128)} %copy.37) | copy-start | bytes 3145732
  40.0 2.3 %copy-start = (f32[1024,512]{1,0:T(8,128)S(1)}, f32[1024,512]{1,0:T(8,128)}, u32[]{:S(2)}) copy-start(f32[1024,512]{1,0:T(8,128)} %copy.47) | copy-start | bytes 6291460
  40.0 2.3 %copy-start.9 = (f32[512]{0:T(512)S(1)}, f32[512]{0:T(512)}, u32[]{:S(2)}) copy-start(f32[512]{0:T(512)} %param.9) | copy-start | bytes 6148
where the time goes:
time: 45.7 us; the launch traced here: 45.2 us
  local copies, waits for them, and re-layouts  14.4 us (32%)
  other arithmetic  9.49 us (21%)
  blocking collectives  9.1 us (20%)
  matrix products  6.53 us (14%)
  starting transfers between devices  4.6 us (10%)
  waiting for transfers between devices  0.77 us (2%)
    all_gather x1, blocking collectives, per_device(): piece = lax.all_gather(packed, 'ctx', axis=0, tiled=True)  9.1 us
    ppermute x2, starting transfers between devices, shifted(): lax.ppermute(value, axis, [(source, source + steps) for source in range(l...  4.6 us
    slice x5, local copies, waits for them, and re-layouts, attend(): summed[begin:begin + size]  3.01 us
    convert_element_type x1, other arithmetic, per_device(): return (normed.reshape(rows, columns) * out_gain).astype(jnp.bfloat16)  2.89 us
    dot_general x2, matrix products, attend(): jnp.einsum('qhk,kd->qhd', weights.astype(jnp.bfloat16), keys[:, HEAD_CHAN...  2.36 us
    mul x1, local copies, waits for them, and re-layouts, per_device(): attended * lax.rsqrt(jnp.mean(attended * attended, -1, keepdims=True) + E...  2.33 us
    reduce_sum x1, other arithmetic, attend(): totals.append(rescale * total[begin:begin + size] + jnp.sum(weights, -1))  2.11 us
    div x2, local copies, waits for them, and re-layouts, per_device(): attended = summed / total[..., None]  2.1 us
  transfers between devices with their start and end apart: 2, of which 1 were waited for; matrix products, arithmetic and copies ran while one was open for 8% of the time, Pallas kernels for 0%

commit v1 on v0

v1 whole, which is shorter than its diff:
```python
import functools
import math

import jax
import jax.numpy as jnp
import numpy as np
from jax import lax
from jax.experimental import pallas as pl
from jax.experimental.pallas import tpu as pltpu
from jax.sharding import PartitionSpec as P

HEAD_CHANNELS = 128
TAPS = 4
TRANSFORM_BLOCK = 128
KEEP = 16
HALO = 16

NEGATIVE = -1e30
EPSILON = 1e-06
MESH = pl.DeviceIdType.MESH


def dct_table():
    frequency = np.arange(KEEP, dtype=np.float32)[:, None]
    offset = np.arange(TRANSFORM_BLOCK, dtype=np.float32)[None, :]
    angle = np.float32(math.pi) * (offset + np.float32(0.5)) * frequency
    table = np.cos(angle / np.float32(TRANSFORM_BLOCK)) * np.float32(
        math.sqrt(2.0 / TRANSFORM_BLOCK)
    )
    table = np.where(frequency == 0.0, table * np.float32(math.sqrt(0.5)), table)
    return table.astype(jnp.bfloat16)


def nt_dot(left, right):
    return lax.dot_general(
        left, right, (((1,), (1,)), ((), ())), preferred_element_type=jnp.float32
    )


def kernel(
    shards,
    per_span,
    heads,
    q_hbm,
    kv_hbm,
    qt_hbm,
    pt_hbm,
    gain_hbm,
    table_hbm,
    out_hbm,
    xq,
    xkv,
    qt,
    pt,
    gain,
    table,
    qc,
    kvc,
    gath,
    out,
    in_sem,
    small_sem,
    own_halo_sem,
    halo_send,
    halo_recv,
    lower_send,
    upper_send,
    gath_recv,
    out_sem,
):
    place = lax.axis_index("ctx")
    block = TRANSFORM_BLOCK
    span_rows = per_span * block
    half = per_span * KEEP
    channels = HEAD_CHANNELS

    loads = {}
    for s in range(2):
        loads["kv", s] = pltpu.make_async_copy(
            kv_hbm.at[pl.ds(s * span_rows, span_rows), :],
            xkv.at[s, pl.ds(HALO, span_rows), :],
            in_sem.at[s],
        )
        loads["q", s] = pltpu.make_async_copy(
            q_hbm.at[pl.ds(s * span_rows, span_rows), :],
            xq.at[s, pl.ds(HALO, span_rows), :],
            in_sem.at[2 + s],
        )
    small = [
        pltpu.make_async_copy(source, target, small_sem.at[n])
        for n, (source, target) in enumerate(
            [(pt_hbm, pt), (table_hbm, table), (qt_hbm, qt), (gain_hbm, gain)]
        )
    ]
    loads["kv", 0].start()
    loads["kv", 1].start()
    for copy in small:
        copy.start()
    loads["q", 0].start()
    loads["q", 1].start()

    barrier = pltpu.get_barrier_semaphore()
    for d in range(1, shards):
        pl.semaphore_signal(
            barrier,
            inc=1,
            device_id={"ctx": lax.rem(place + d, shards)},
            device_id_type=MESH,
        )
    pl.semaphore_wait(barrier, shards - 1)

    def halo_copy(n, s, step):
        source, target = ((kv_hbm, xkv), (q_hbm, xq))[n]
        return pltpu.make_async_remote_copy(
            src_ref=source.at[pl.ds((s + 1) * span_rows - HALO, HALO), :],
            dst_ref=target.at[s, pl.ds(0, HALO), :],
            send_sem=halo_send.at[n, s],
            recv_sem=halo_recv.at[n, s],
            device_id={"ctx": lax.rem(place + step + shards, shards)},
            device_id_type=MESH,
        )

    def own_halo(n):
        source, target = ((kv_hbm, xkv), (q_hbm, xq))[n]
        return pltpu.make_async_copy(
            source.at[pl.ds(span_rows - HALO, HALO), :],
            target.at[1, pl.ds(0, HALO), :],
            own_halo_sem.at[n],
        )

    first = place == 0
    last = place == shards - 1
    for n in range(2):

        @pl.when(jnp.logical_not(last))
        def _():
            halo_copy(n, 0, 1).start()

        @pl.when(jnp.logical_not(first))
        def _():
            halo_copy(n, 1, -1).start()

        @pl.when(last)
        def _():
            own_halo(n).start()

    @pl.when(first)
    def _():
        xkv[0, :HALO, :] = jnp.zeros((HALO, xkv.shape[2]), xkv.dtype)
        xq[0, :HALO, :] = jnp.zeros((HALO, xq.shape[2]), xq.dtype)

    for q in range(shards - 1):

        @pl.when(q < place)
        def _():
            gath[2 * shards - 1 - q] = jnp.zeros(gath.shape[1:], gath.dtype)

    def wait_halo(n):
        @pl.when(jnp.logical_not(first))
        def _():
            halo_copy(n, 0, 1).wait_recv()

        @pl.when(jnp.logical_not(last))
        def _():
            halo_copy(n, 1, -1).wait_recv()

        @pl.when(last)
        def _():
            own_halo(n).wait()

    def conv(source, s, i, taps, g):
        columns = pl.ds(g * channels, channels)
        rows = pl.ds(pl.multiple_of(i * block, block), block + HALO)
        x = source[s, rows, columns].astype(jnp.float32)
        w = taps[:, columns]
        total = w[0:1] * x[HALO:]
        for shift in range(1, TAPS):
            total = total + w[shift : shift + 1] * pltpu.roll(x, shift, 0)[HALO:]
        return total.astype(jnp.bfloat16)

    spans = (place, 2 * shards - 1 - place)

    def pair_block(s, i):
        for g in range(2):
            kvc[s * per_span + i, :, g * channels : (g + 1) * channels] = conv(
                xkv, s, i, pt, g
            )
        packed = jnp.dot(
            table[...], kvc[s * per_span + i], preferred_element_type=jnp.float32
        )
        gath[spans[s], pl.ds(pl.multiple_of(i * KEEP, KEEP), KEEP), :] = packed.astype(
            jnp.bfloat16
        )

    def query_block(s, i):
        for h in range(heads):
            qc[s * per_span + i, h] = conv(xq, s, i, qt, h)

    def loop(low, high, body):
        def step(i, carry):
            body(i)
            return carry

        lax.fori_loop(low, high, step, 0)

    small[0].wait()
    small[1].wait()
    for s in range(2):
        loads["kv", s].wait()
        loop(1, per_span, functools.partial(pair_block, s))
    wait_halo(0)
    for s in range(2):
        pair_block(s, 0)

    def span_copy(s, target):
        return pltpu.make_async_remote_copy(
            src_ref=gath.at[spans[s]],
            dst_ref=gath.at[spans[s]],
            send_sem=(lower_send, upper_send)[s].at[target],
            recv_sem=gath_recv.at[spans[s]],
            device_id={"ctx": target},
            device_id_type=MESH,
        )

    for d in range(1, shards):
        span_copy(0, lax.rem(place + d, shards)).start()
    for q in range(shards - 1):

        @pl.when(q < place)
        def _():
            span_copy(1, q).start()

    small[2].wait()
    small[3].wait()
    for s in range(2):
        loads["q", s].wait()
        loop(1, per_span, functools.partial(query_block, s))
    wait_halo(1)
    for s in range(2):
        query_block(s, 0)

    def arrived(span):
        return pltpu.make_async_remote_copy(
            src_ref=gath.at[span],
            dst_ref=gath.at[span],
            send_sem=lower_send.at[0],
            recv_sem=gath_recv.at[span],
            device_id={"ctx": lax.rem(place + 1, shards)},
            device_id_type=MESH,
        )

    scale = math.log2(math.e) / math.sqrt(channels)
    row_id = lax.broadcasted_iota(jnp.int32, (block, block), 0)
    column_id = lax.broadcasted_iota(jnp.int32, (block, block), 1)

    def out_copy(s, i):
        rows = pl.ds(pl.multiple_of((s * per_span + i) * block, block), block)
        return pltpu.make_async_copy(
            out.at[rows, :], out_hbm.at[rows, :], out_sem.at[s * per_span + i]
        )

    def attend(s, i):
        index = s * per_span + i
        far_rows = (s + 1) * shards * half
        query = qc[index].reshape(heads * block, channels)
        near = kvc[index]
        far = gath[: (s + 1) * shards].reshape(far_rows, 2 * channels)
        seen = (spans[s] * per_span + i) * KEEP
        near_bias = jnp.where(row_id >= column_id, 0.0, NEGATIVE)
        far_bias = jnp.where(
            lax.broadcasted_iota(jnp.int32, (1, far_rows), 1) < seen, 0.0, NEGATIVE
        )
        near_scores = nt_dot(query, near[:, :channels])
        near_scores = (
            near_scores.reshape(heads, block, block) + near_bias[None]
        ).reshape(heads * block, block)
        far_scores = nt_dot(query, far[:, :channels]) + far_bias
        scores = jnp.concatenate([near_scores, far_scores], 1)
        top = jnp.max(scores, -1, keepdims=True)
        weights = jnp.exp2((scores - top) * scale).astype(jnp.bfloat16)
        values = jnp.concatenate([near[:, channels:], far[:, channels:]], 0)
        values = jnp.concatenate([values, jnp.ones_like(values)], 1)
        both = jnp.dot(weights, values, preferred_element_type=jnp.float32)
        summed, total = both[:, :channels], both[:, channels:]
        mean = jnp.mean(summed * summed, -1, keepdims=True)
        normed = summed * lax.rsqrt(mean + EPSILON * (total * total))
        rows = pl.ds(pl.multiple_of(index * block, block), block)
        for h in range(heads):
            columns = pl.ds(h * channels, channels)
            out[rows, columns] = (
                normed[h * block : (h + 1) * block] * gain[:, columns]
            ).astype(jnp.bfloat16)
        out_copy(s, i).start()

    for q in range(shards):

        @pl.when(q != place)
        def _():
            arrived(q).wait_recv()

    loop(0, per_span, functools.partial(attend, 0))
    for q in range(1, shards):

        @pl.when(q > place)
        def _():
            arrived(2 * shards - 1 - q).wait_recv()

    loop(0, per_span, functools.partial(attend, 1))

    for s in range(2):
        loop(0, per_span, lambda i: out_copy(s, i).wait())
    for n in range(2):

        @pl.when(jnp.logical_not(last))
        def _():
            halo_copy(n, 0, 1).wait_send()

        @pl.when(jnp.logical_not(first))
        def _():
            halo_copy(n, 1, -1).wait_send()

    for d in range(1, shards):
        span_copy(0, lax.rem(place + d, shards)).wait_send()
    for q in range(shards - 1):

        @pl.when(q < place)
        def _():
            span_copy(1, q).wait_send()


def attention(queries, pairs, query_taps, pair_taps, out_gain, shards):
    rows, columns = queries.shape
    span_rows = rows // 2
    per_span = span_rows // TRANSFORM_BLOCK
    heads = columns // HEAD_CHANNELS
    half = per_span * KEEP
    blocks = 2 * per_span
    bf16, f32 = jnp.bfloat16, jnp.float32
    width = 2 * HEAD_CHANNELS
    anywhere = pl.BlockSpec(memory_space=pl.ANY)
    dma = pltpu.SemaphoreType.DMA
    return pl.pallas_call(
        functools.partial(kernel, shards, per_span, heads),
        out_shape=jax.ShapeDtypeStruct((rows, columns), bf16),
        in_specs=[anywhere] * 6,
        out_specs=anywhere,
        scratch_shapes=[
            pltpu.VMEM((2, HALO + span_rows, columns), bf16),
            pltpu.VMEM((2, HALO + span_rows, width), bf16),
            pltpu.VMEM((TAPS, columns), f32),
            pltpu.VMEM((TAPS, width), f32),
            pltpu.VMEM((1, columns), f32),
            pltpu.VMEM((KEEP, TRANSFORM_BLOCK), bf16),
            pltpu.VMEM((blocks, heads, TRANSFORM_BLOCK, HEAD_CHANNELS), bf16),
            pltpu.VMEM((blocks, TRANSFORM_BLOCK, width), bf16),
            pltpu.VMEM((2 * shards, half, width), bf16),
            pltpu.VMEM((rows, columns), bf16),
            dma((4,)),
            dma((4,)),
            dma((2,)),
            dma((2, 2)),
            dma((2, 2)),
            dma((shards,)),
            dma((shards,)),
            dma((2 * shards,)),
            dma((blocks,)),
        ],
        compiler_params=pltpu.CompilerParams(
            collective_id=0, has_side_effects=True, vmem_limit_bytes=48 * 1024 * 1024
        ),
        name="conv_attention",
    )(
        queries,
        pairs,
        query_taps,
        pair_taps,
        out_gain.reshape(1, columns),
        jnp.asarray(dct_table()),
    )


def from_partner(block, axis, apart):
    count = lax.axis_size(axis)
    route = []
    for low in range(count):
        high = low | 1 << apart
        if high != low and high < count:
            route += [(low, high), (high, low)]
    return lax.ppermute(block, axis, route)


def per_device(queries, keys_values, query_taps, pair_taps, out_gain):
    member = lax.axis_index("mp")
    width = keys_values.shape[1]
    rounds = (2 * HEAD_CHANNELS // width).bit_length() - 1

    def join(mine, bit):
        other = from_partner(mine, "mp", bit)
        lower = member // 2**bit % 2 == 0
        return jnp.where(
            lower, jnp.concatenate([mine, other], 1), jnp.concatenate([other, mine], 1)
        )

    for bit in range(rounds):
        keys_values = join(keys_values, bit)
        pair_taps = join(pair_taps, bit)
    return attention(
        queries, keys_values, query_taps, pair_taps, out_gain, lax.axis_size("ctx")
    )


def solution(mesh):
    in_specs = (P("ctx", "mp"), P("ctx", "mp"), P(None, "mp"), P(None, "mp"), P("mp"))
    out_specs = P("ctx", "mp")
    return jax.shard_map(
        per_device, mesh=mesh, in_specs=in_specs, out_specs=out_specs, check_vma=False
    )
```

time: 45.7 us -> 23.4 us (0.51)
  Pallas kernels: 0 us -> 17.1 us
  other arithmetic: 9.49 us -> 0 us
  blocking collectives: 9.1 us -> 0 us
  local copies, waits for them, and re-layouts: 14.4 us -> 5.99 us
  matrix products: 6.53 us -> 0 us
  starting transfers between devices: 4.6 us -> 0 us
  waiting for transfers between devices: 0.77 us -> 0 us
    pallas_call x0 -> x1, Pallas kernels: none -> 17.1 us  [attention(): pl.pallas_call(functools.partial(kernel, shards, per_span, heads), out_sh...]
    all_gather x1 -> x0, blocking collectives: 9.1 us -> none  [per_device(): piece = lax.all_gather(packed, 'ctx', axis=0, tiled=True)]
    slice x16 -> x0, local copies, waits for them, and re-layouts: 6.85 us -> none  [the longest x5 3.01 us: attend(): summed[begin:begin + size]]
    dot_general x7 -> x0, matrix products: 6.53 us -> none  [the longest x2 2.36 us: attend(): jnp.einsum('qhk,kd->qhd', weights.astype(jnp.bfloat16), keys[:, HEAD_CHAN...]
    unnamed x20 -> x13, local copies, waits for them, and re-layouts: 0.13 us -> 5.99 us
    ppermute x2 -> x0, starting transfers between devices: 4.6 us -> none  [shifted(): lax.ppermute(value, axis, [(source, source + steps) for source in range(l...]
    convert_element_type x3 -> x0, other arithmetic: 4.39 us -> none  [the longest x1 2.89 us: per_device(): return (normed.reshape(rows, columns) * out_gain).astype(jnp.bfloat16)]
    reduce_sum x3 -> x0, other arithmetic: 2.97 us -> none  [the longest x1 2.11 us: attend(): totals.append(rescale * total[begin:begin + size] + jnp.sum(weights, -1))]
  transfers between devices with their start and end apart: 2 -> 0, of which waited for: 1 -> 0; matrix products, arithmetic and copies ran while one was open for 8% -> 0% of each run, Pallas kernels for 0% -> 0%
where the time goes in v1:
time: 23.4 us; the launch traced here: 23.1 us
  Pallas kernels  17.1 us (73%)
  local copies, waits for them, and re-layouts  5.99 us (26%)
    pallas_call x1, Pallas kernels, attention(): pl.pallas_call(functools.partial(kernel, shards, per_span, heads), out_sh...  17.1 us
    unnamed x13, local copies, waits for them, and re-layouts  5.99 us

profile of v1, /device:TPU:0, one launch (start us, length us, event | category | flops | bytes accessed | tf_op | source)
XLA Modules:
  0.0 23.1 jit_solution(6146770723204267744)
XLA Ops:
  0.0 0.0 copy-start
  0.0 1.2 %copy-done = bf16[1024,512]{1,0:T(8,128)(2,1)S(1)} copy-done((bf16[1024,512]{1,0:T(8,128)(2,1)S(1)}, bf16[1024,512]{1,0:T(8,128)(2,1)}, u32[]{:S(2)}) %copy-start) | copy-done | bytes 1048600
  1.2 0.0 copy-start.1
  1.2 1.0 %copy-done.1 = bf16[1024,256]{1,0:T(8,128)(2,1)S(1)} copy-done((bf16[1024,256]{1,0:T(8,128)(2,1)S(1)}, bf16[1024,256]{1,0:T(8,128)(2,1)}, u32[]{:S(2)}) %copy-start.1) | copy-done | bytes 524312
  2.3 0.0 copy-start.2
  2.3 0.7 %copy-done.2 = f32[4,512]{1,0:T(4,128)S(1)} copy-done((f32[4,512]{1,0:T(4,128)S(1)}, f32[4,512]{1,0:T(4,128)}, u32[]{:S(2)}) %copy-start.2) | copy-done | bytes 8216
  3.0 0.0 copy-start.3
  3.0 0.7 %copy-done.3 = f32[4,256]{1,0:T(4,128)S(1)} copy-done((f32[4,256]{1,0:T(4,128)S(1)}, f32[4,256]{1,0:T(4,128)}, u32[]{:S(2)}) %copy-start.3) | copy-done | bytes 4120
  3.7 0.0 copy-start.4
  3.7 0.7 %copy-done.4 = bf16[16,128]{1,0:T(8,128)(2,1)S(1)} copy-done((bf16[16,128]{1,0:T(8,128)(2,1)S(1)}, bf16[16,128]{1,0:T(8,128)(2,1)}, u32[]{:S(2)}) %copy-start.4) | copy-done | bytes 4120
  4.3 0.0 copy-start.5
  4.3 0.7 %copy-done.5 = f32[512]{0:T(512)S(1)} copy-done((f32[512]{0:T(512)S(1)}, f32[512]{0:T(512)}, u32[]{:S(2)}) %copy-start.5) | copy-done | bytes 2072
  5.0 17.1 %conv_attention.1 = bf16[1024,512]{1,0:T(8,128)(2,1)S(1)} custom-call(bf16[1024,512]{1,0:T(8,128)(2,1)S(1)} %copy-done, bf16[1024,256]{1,0:T(8,128)(2,1)S(1)} %copy-done.1, f32[4,512]{1,0:T(4,128)S(1)} %copy-done.2, f32[4,256]{1,0:T(4,128)S(1)} %copy-done.3, f32[1,512]{1,0:T(1,128)S(1)} %bitcast.1, bf16[16,128]{1,0:T(8,128)(2,1)S(1)} %copy-done.4), custom_call_target="tpu_custom_call" | custom-call | tf_op jit(solution)/shard_map/conv_attention/pallas_call | solution.py:342
  22.1 1.0 %copy.8 = bf16[1024,512]{1,0:T(8,128)(2,1)} copy(bf16[1024,512]{1,0:T(8,128)(2,1)S(1)} %conv_attention.1) | data formatting | bytes 2097152
Async XLA Ops:
  0.0 1.2 %copy-start = (bf16[1024,512]{1,0:T(8,128)(2,1)S(1)}, bf16[1024,512]{1,0:T(8,128)(2,1)}, u32[]{:S(2)}) copy-start(bf16[1024,512]{1,0:T(8,128)(2,1)} %q_hbm.1) | copy-start | bytes 3145732
  1.2 1.0 %copy-start.1 = (bf16[1024,256]{1,0:T(8,128)(2,1)S(1)}, bf16[1024,256]{1,0:T(8,128)(2,1)}, u32[]{:S(2)}) copy-start(bf16[1024,256]{1,0:T(8,128)(2,1)} %kv_hbm.1) | copy-start | bytes 1572868
  2.3 0.7 %copy-start.2 = (f32[4,512]{1,0:T(4,128)S(1)}, f32[4,512]{1,0:T(4,128)}, u32[]{:S(2)}) copy-start(f32[4,512]{1,0:T(4,128)} %qt_hbm.1) | copy-start | bytes 24580
  3.0 0.7 %copy-start.3 = (f32[4,256]{1,0:T(4,128)S(1)}, f32[4,256]{1,0:T(4,128)}, u32[]{:S(2)}) copy-start(f32[4,256]{1,0:T(4,128)} %pt_hbm.1) | copy-start | bytes 12292
  3.7 0.7 %copy-start.4 = (bf16[16,128]{1,0:T(8,128)(2,1)S(1)}, bf16[16,128]{1,0:T(8,128)(2,1)}, u32[]{:S(2)}) copy-start(bf16[16,128]{1,0:T(8,128)(2,1)} %constant.2.clone.table_hbm) | copy-start | bytes 12292
  4.3 0.7 %copy-start.5 = (f32[512]{0:T(512)S(1)}, f32[512]{0:T(512)}, u32[]{:S(2)}) copy-start(f32[512]{0:T(512)} %param.10) | copy-start | bytes 6148

commit v2 on v1

--- a/solution.py
+++ b/solution.py
@@ -14,6 +14,7 @@
 TRANSFORM_BLOCK = 128
 KEEP = 16
 HALO = 16
+FAR_PARTS = 4
 
 NEGATIVE = -1e30
 EPSILON = 1e-06
@@ -45,7 +46,7 @@
     kv_hbm,
     qt_hbm,
     pt_hbm,
-    gain_hbm,
+    gahbm,
     table_hbm,
     out_hbm,
     xq,
@@ -66,6 +67,9 @@
     lower_send,
     upper_send,
     gath_recv,
+    lower_first,
+    upper_first,
+    first_recv,
     out_sem,
 ):
     place = lax.axis_index("ctx")
@@ -89,7 +93,7 @@
     small = [
         pltpu.make_async_copy(source, target, small_sem.at[n])
         for n, (source, target) in enumerate(
-            [(pt_hbm, pt), (table_hbm, table), (qt_hbm, qt), (gain_hbm, gain)]
+            [(pt_hbm, pt), (table_hbm, table), (qt_hbm, qt), (gahbm, gain)]
         )
     ]
     loads["kv", 0].start()
@@ -173,10 +177,11 @@
         rows = pl.ds(pl.multiple_of(i * block, block), block + HALO)
         x = source[s, rows, columns].astype(jnp.float32)
         w = taps[:, columns]
-        total = w[0:1] * x[HALO:]
-        for shift in range(1, TAPS):
-            total = total + w[shift : shift + 1] * pltpu.roll(x, shift, 0)[HALO:]
-        return total.astype(jnp.bfloat16)
+        back = pltpu.roll(x, 1, 0)
+        newer = w[0:1] * x[HALO:] + w[1:2] * back[HALO:]
+        older = w[2:3] * x[HALO // 2 :] + w[3:4] * back[HALO // 2 :]
+        older = pltpu.roll(older, 2, 0)[HALO // 2 :]
+        return (newer + older).astype(jnp.bfloat16)
 
     spans = (place, 2 * shards - 1 - place)
 
@@ -208,27 +213,39 @@
     for s in range(2):
         loads["kv", s].wait()
         loop(1, per_span, functools.partial(pair_block, s))
+
+    def span_copy(s, span, target, part):
+        rows = (pl.ds(0, KEEP), pl.ds(KEEP, half - KEEP))[part]
+        send = ((lower_first, lower_send), (upper_first, upper_send))[s][part]
+        return pltpu.make_async_remote_copy(
+            src_ref=gath.at[span, rows, :],
+            dst_ref=gath.at[span, rows, :],
+            send_sem=send.at[target],
+            recv_sem=(first_recv, gath_recv)[part].at[span],
+            device_id={"ctx": target},
+            device_id_type=MESH,
+        )
+
+    def for_each_target(part, act):
+        for q in range(shards - 1):
+
+            @pl.when(q < place)
+            def _():
+                act(span_copy(1, spans[1], q, part))
+
+        for d in range(1, shards):
+            act(span_copy(0, spans[0], lax.rem(place + d, shards), part))
+
+    def arrive(s, q):
+        span = (q, 2 * shards - 1 - q)[s]
+        for part in range(2):
+            span_copy(s, span, lax.rem(place + 1, shards), part).wait_recv()
+
+    for_each_target(1, lambda copy: copy.start())
     wait_halo(0)
     for s in range(2):
         pair_block(s, 0)
-
-    def span_copy(s, target):
-        return pltpu.make_async_remote_copy(
-            src_ref=gath.at[spans[s]],
-            dst_ref=gath.at[spans[s]],
-            send_sem=(lower_send, upper_send)[s].at[target],
-            recv_sem=gath_recv.at[spans[s]],
-            device_id={"ctx": target},
-            device_id_type=MESH,
-        )
-
-    for d in range(1, shards):
-        span_copy(0, lax.rem(place + d, shards)).start()
-    for q in range(shards - 1):
-
-        @pl.when(q < place)
-        def _():
-            span_copy(1, q).start()
+    for_each_target(0, lambda copy: copy.start())
 
     small[2].wait()
     small[3].wait()
@@ -239,43 +256,31 @@
     for s in range(2):
         query_block(s, 0)
 
-    def arrived(span):
-        return pltpu.make_async_remote_copy(
-            src_ref=gath.at[span],
-            dst_ref=gath.at[span],
-            send_sem=lower_send.at[0],
-            recv_sem=gath_recv.at[span],
-            device_id={"ctx": lax.rem(place + 1, shards)},
-            device_id_type=MESH,
-        )
-
     scale = math.log2(math.e) / math.sqrt(channels)
     row_id = lax.broadcasted_iota(jnp.int32, (block, block), 0)
     column_id = lax.broadcasted_iota(jnp.int32, (block, block), 1)
 
-    def out_copy(s, i):
-        rows = pl.ds(pl.multiple_of((s * per_span + i) * block, block), block)
-        return pltpu.make_async_copy(
-            out.at[rows, :], out_hbm.at[rows, :], out_sem.at[s * per_span + i]
-        )
-
-    def attend(s, i):
-        index = s * per_span + i
-        far_rows = (s + 1) * shards * half
+    part_rows = 2 * shards * half // FAR_PARTS
+
+    def attend(index, parts):
+        far_rows = parts * part_rows
         query = qc[index].reshape(heads * block, channels)
         near = kvc[index]
-        far = gath[: (s + 1) * shards].reshape(far_rows, 2 * channels)
-        seen = (spans[s] * per_span + i) * KEEP
+        far = gath[: far_rows // half].reshape(far_rows, 2 * channels)
         near_bias = jnp.where(row_id >= column_id, 0.0, NEGATIVE)
+        far_ids = lax.broadcasted_iota(jnp.int32, (1, part_rows), 1)
         far_bias = jnp.where(
-            lax.broadcasted_iota(jnp.int32, (1, far_rows), 1) < seen, 0.0, NEGATIVE
+            far_ids + (far_rows - part_rows) < block_id(index) * KEEP, 0.0, NEGATIVE
         )
         near_scores = nt_dot(query, near[:, :channels])
         near_scores = (
             near_scores.reshape(heads, block, block) + near_bias[None]
         ).reshape(heads * block, block)
-        far_scores = nt_dot(query, far[:, :channels]) + far_bias
-        scores = jnp.concatenate([near_scores, far_scores], 1)
+        far_scores = nt_dot(query, far[:, :channels])
+        pieces = [near_scores, far_scores[:, far_rows - part_rows :] + far_bias]
+        if parts > 1:
+            pieces.insert(1, far_scores[:, : far_rows - part_rows])
+        scores = jnp.concatenate(pieces, 1)
         top = jnp.max(scores, -1, keepdims=True)
         weights = jnp.exp2((scores - top) * scale).astype(jnp.bfloat16)
         values = jnp.concatenate([near[:, channels:], far[:, channels:]], 0)
@@ -290,25 +295,46 @@
             out[rows, columns] = (
                 normed[h * block : (h + 1) * block] * gain[:, columns]
             ).astype(jnp.bfloat16)
-        out_copy(s, i).start()
+
+        out_copy(index).start()
+
+    def out_copy(index):
+        rows = pl.ds(pl.multiple_of(index * block, block), block)
+        return pltpu.make_async_copy(
+            out.at[rows, :], out_hbm.at[rows, :], out_sem.at[index]
+        )
+
+    def block_id(index):
+        upper = index // per_span
+        span = place + upper * (2 * shards - 1 - 2 * place)
+        return span * per_span + lax.rem(index, per_span)
 
     for q in range(shards):
 
         @pl.when(q != place)
         def _():
-            arrived(q).wait_recv()
-
-    loop(0, per_span, functools.partial(attend, 0))
-    for q in range(1, shards):
-
-        @pl.when(q > place)
-        def _():
-            arrived(2 * shards - 1 - q).wait_recv()
-
-    loop(0, per_span, functools.partial(attend, 1))
-
-    for s in range(2):
-        loop(0, per_span, lambda i: out_copy(s, i).wait())
+            arrive(0, q)
+
+    def step(index):
+        @pl.when(index == per_span)
+        def _():
+            for q in range(1, shards):
+
+                @pl.when(q > place)
+                def _():
+                    arrive(1, q)
+
+        needed = (block_id(index) * KEEP + part_rows - 1) // part_rows
+        for parts in range(1, FAR_PARTS + 1):
+            fits = needed <= 1 if parts == 1 else needed == parts
+
+            @pl.when(fits)
+            def _():
+                attend(index, parts)
+
+    loop(0, 2 * per_span, step)
+    loop(0, 2 * per_span, lambda index: out_copy(index).wait())
+
     for n in range(2):
 
         @pl.when(jnp.logical_not(last))
@@ -319,13 +345,8 @@
         def _():
             halo_copy(n, 1, -1).wait_send()
 
-    for d in range(1, shards):
-        span_copy(0, lax.rem(place + d, shards)).wait_send()
-    for q in range(shards - 1):
-
-        @pl.when(q < place)
-        def _():
-            span_copy(1, q).wait_send()
+    for part in range(2):
+        for_each_target(part, lambda copy: copy.wait_send())
 
 
 def attention(queries, pairs, query_taps, pair_taps, out_gain, shards):
@@ -337,13 +358,13 @@
     blocks = 2 * per_span
     bf16, f32 = jnp.bfloat16, jnp.float32
     width = 2 * HEAD_CHANNELS
-    anywhere = pl.BlockSpec(memory_space=pl.ANY)
+    hbm = pl.BlockSpec(memory_space=pltpu.HBM)
     dma = pltpu.SemaphoreType.DMA
     return pl.pallas_call(
         functools.partial(kernel, shards, per_span, heads),
         out_shape=jax.ShapeDtypeStruct((rows, columns), bf16),
-        in_specs=[anywhere] * 6,
-        out_specs=anywhere,
+        in_specs=[hbm] * 6,
+        out_specs=hbm,
         scratch_shapes=[
             pltpu.VMEM((2, HALO + span_rows, columns), bf16),
             pltpu.VMEM((2, HALO + span_rows, width), bf16),
@@ -363,10 +384,13 @@
             dma((shards,)),
             dma((shards,)),
             dma((2 * shards,)),
+            dma((shards,)),
+            dma((shards,)),
+            dma((2 * shards,)),
             dma((blocks,)),
         ],
         compiler_params=pltpu.CompilerParams(
-            collective_id=0, has_side_effects=True, vmem_limit_bytes=48 * 1024 * 1024
+            collective_id=0, has_side_effects=True, vmem_limit_bytes=62 * 1024 * 1024
         ),
         name="conv_attention",
     )(

time: 23.4 us -> 19.3 us (0.82)
  local copies, waits for them, and re-layouts: 5.99 us -> 2.26 us
    unnamed x13 -> x1, local copies, waits for them, and re-layouts: 5.99 us -> 2.26 us
where the time goes in v2:
time: 19.3 us; the launch traced here: 19.2 us
  Pallas kernels  16.9 us (88%)
  local copies, waits for them, and re-layouts  2.26 us (12%)
    pallas_call x1, Pallas kernels, attention(): pl.pallas_call(functools.partial(kernel, shards, per_span, heads), out_sh...  16.9 us
    unnamed x1, local copies, waits for them, and re-layouts  2.26 us

profile of v2, /device:TPU:0, one launch (start us, length us, event | category | flops | bytes accessed | tf_op | source)
XLA Modules:
  0.0 19.2 jit_solution(2044551386970070295)
XLA Ops:
  0.0 16.9 %conv_attention.1 = bf16[1024,512]{1,0:T(8,128)(2,1)} custom-call(bf16[1024,512]{1,0:T(8,128)(2,1)} %q_hbm.1, bf16[1024,256]{1,0:T(8,128)(2,1)} %kv_hbm.1, f32[4,512]{1,0:T(4,128)} %qt_hbm.1, f32[4,256]{1,0:T(4,128)} %pt_hbm.1, f32[1,512]{1,0:T(1,128)} %bitcast.1, bf16[16,128]{1,0:T(8,128)(2,1)} %constant.2.clone.table_hbm), custom_call_target="tpu_custom_call" | custom-call | tf_op jit(solution)/shard_map/conv_attention/pallas_call | solution.py:363
  16.9 2.3 %copy.8 = bf16[1024,512]{1,0:T(8,128)(2,1)} copy(bf16[1024,512]{1,0:T(8,128)(2,1)} %conv_attention.1) | data formatting | bytes 2097152

commit v3 on v2

--- a/solution.py
+++ b/solution.py
@@ -64,12 +64,8 @@
     own_halo_sem,
     halo_send,
     halo_recv,
-    lower_send,
-    upper_send,
-    gath_recv,
-    lower_first,
-    upper_first,
-    first_recv,
+    span_send,
+    span_recv,
     out_sem,
 ):
     place = lax.axis_index("ctx")
@@ -214,38 +210,59 @@
         loads["kv", s].wait()
         loop(1, per_span, functools.partial(pair_block, s))
 
-    def span_copy(s, span, target, part):
+    mate = place + 1 - 2 * lax.rem(place, 2)
+    chips = shards // 2
+
+    def peer(d):
+        return lax.rem(place + 2 * d, shards)
+
+    def span_copy(s, span, target, part, hop):
         rows = (pl.ds(0, KEEP), pl.ds(KEEP, half - KEEP))[part]
-        send = ((lower_first, lower_send), (upper_first, upper_send))[s][part]
         return pltpu.make_async_remote_copy(
             src_ref=gath.at[span, rows, :],
             dst_ref=gath.at[span, rows, :],
-            send_sem=send.at[target],
-            recv_sem=(first_recv, gath_recv)[part].at[span],
+            send_sem=span_send.at[part, s, hop],
+            recv_sem=span_recv.at[part, span],
             device_id={"ctx": target},
             device_id_type=MESH,
         )
 
-    def for_each_target(part, act):
-        for q in range(shards - 1):
-
-            @pl.when(q < place)
-            def _():
-                act(span_copy(1, spans[1], q, part))
-
-        for d in range(1, shards):
-            act(span_copy(0, spans[0], lax.rem(place + d, shards), part))
-
-    def arrive(s, q):
+    def when(condition, act):
+        @pl.when(condition)
+        def _():
+            act()
+
+    def own_copies(part, act):
+        for d in range(1, chips):
+            target = peer(d)
+            act(span_copy(0, spans[0], target, part, d))
+            when(target < place, lambda: act(span_copy(1, spans[1], target, part, d)))
+        act(span_copy(0, spans[0], mate, part, 0))
+        when(mate < place, lambda: act(span_copy(1, spans[1], mate, part, 0)))
+
+    def passed_copies(part, d, act):
+        source = peer(d)
+        hop = chips - 1 + d
+        act(span_copy(0, source, mate, part, hop))
+        upper = 2 * shards - 1 - source
+        when(source > place, lambda: act(span_copy(1, upper, mate, part, hop)))
+
+    def arrive(s, q, part):
         span = (q, 2 * shards - 1 - q)[s]
-        for part in range(2):
-            span_copy(s, span, lax.rem(place + 1, shards), part).wait_recv()
-
-    for_each_target(1, lambda copy: copy.start())
+        span_copy(s, span, mate, part, 0).wait_recv()
+
+    def pass_on(part):
+        for d in range(1, chips):
+            source = peer(d)
+            arrive(0, source, part)
+            when(source > place, lambda: arrive(1, source, part))
+            passed_copies(part, d, lambda copy: copy.start())
+
+    own_copies(1, lambda copy: copy.start())
     wait_halo(0)
     for s in range(2):
         pair_block(s, 0)
-    for_each_target(0, lambda copy: copy.start())
+    own_copies(0, lambda copy: copy.start())
 
     small[2].wait()
     small[3].wait()
@@ -264,7 +281,6 @@
 
     def attend(index, parts):
         far_rows = parts * part_rows
-        query = qc[index].reshape(heads * block, channels)
         near = kvc[index]
         far = gath[: far_rows // half].reshape(far_rows, 2 * channels)
         near_bias = jnp.where(row_id >= column_id, 0.0, NEGATIVE)
@@ -272,30 +288,32 @@
         far_bias = jnp.where(
             far_ids + (far_rows - part_rows) < block_id(index) * KEEP, 0.0, NEGATIVE
         )
-        near_scores = nt_dot(query, near[:, :channels])
-        near_scores = (
-            near_scores.reshape(heads, block, block) + near_bias[None]
-        ).reshape(heads * block, block)
-        far_scores = nt_dot(query, far[:, :channels])
-        pieces = [near_scores, far_scores[:, far_rows - part_rows :] + far_bias]
-        if parts > 1:
-            pieces.insert(1, far_scores[:, : far_rows - part_rows])
-        scores = jnp.concatenate(pieces, 1)
-        top = jnp.max(scores, -1, keepdims=True)
-        weights = jnp.exp2((scores - top) * scale).astype(jnp.bfloat16)
         values = jnp.concatenate([near[:, channels:], far[:, channels:]], 0)
         values = jnp.concatenate([values, jnp.ones_like(values)], 1)
-        both = jnp.dot(weights, values, preferred_element_type=jnp.float32)
-        summed, total = both[:, :channels], both[:, channels:]
-        mean = jnp.mean(summed * summed, -1, keepdims=True)
-        normed = summed * lax.rsqrt(mean + EPSILON * (total * total))
         rows = pl.ds(pl.multiple_of(index * block, block), block)
-        for h in range(heads):
-            columns = pl.ds(h * channels, channels)
-            out[rows, columns] = (
-                normed[h * block : (h + 1) * block] * gain[:, columns]
-            ).astype(jnp.bfloat16)
-
+        some = min(heads, 2)
+        for begin in range(0, heads, some):
+            query = qc[index, begin : begin + some].reshape(some * block, channels)
+            near_scores = nt_dot(query, near[:, :channels])
+            near_scores = (
+                near_scores.reshape(some, block, block) + near_bias[None]
+            ).reshape(some * block, block)
+            far_scores = nt_dot(query, far[:, :channels])
+            pieces = [near_scores, far_scores[:, far_rows - part_rows :] + far_bias]
+            if parts > 1:
+                pieces.insert(1, far_scores[:, : far_rows - part_rows])
+            scores = jnp.concatenate(pieces, 1)
+            top = jnp.max(scores, -1, keepdims=True)
+            weights = jnp.exp2((scores - top) * scale).astype(jnp.bfloat16)
+            both = jnp.dot(weights, values, preferred_element_type=jnp.float32)
+            summed, total = both[:, :channels], both[:, channels:]
+            mean = jnp.mean(summed * summed, -1, keepdims=True)
+            normed = summed * lax.rsqrt(mean + EPSILON * (total * total))
+            for h in range(some):
+                columns = pl.ds((begin + h) * channels, channels)
+                out[rows, columns] = (
+                    normed[h * block : (h + 1) * block] * gain[:, columns]
+                ).astype(jnp.bfloat16)
         out_copy(index).start()
 
     def out_copy(index):
@@ -309,22 +327,36 @@
         span = place + upper * (2 * shards - 1 - 2 * place)
         return span * per_span + lax.rem(index, per_span)
 
-    for q in range(shards):
-
-        @pl.when(q != place)
-        def _():
-            arrive(0, q)
+    def from_mate(s, q):
+        return jnp.logical_and(
+            lax.rem(q, 2) == lax.rem(mate, 2), (q >= 0) if s == 0 else (q > place)
+        )
+
+    def needed_parts(index):
+        return (block_id(index) * KEEP + part_rows - 1) // part_rows
+
+    lower_spans = needed_parts(per_span - 1) * (part_rows // half)
+
+    def await_spans(s, low, high):
+        for q in range(shards):
+            wanted = jnp.logical_and(q >= low, q < high)
+
+            @pl.when(jnp.logical_and(wanted, from_mate(s, q)))
+            def _():
+                for part in range(2):
+                    arrive(s, q, part)
+
+    pass_on(1)
+    pass_on(0)
+    await_spans(0, 0, lower_spans)
 
     def step(index):
         @pl.when(index == per_span)
         def _():
-            for q in range(1, shards):
-
-                @pl.when(q > place)
-                def _():
-                    arrive(1, q)
-
-        needed = (block_id(index) * KEEP + part_rows - 1) // part_rows
+            await_spans(0, lower_spans, shards)
+            await_spans(1, 0, shards)
+
+        needed = needed_parts(index)
         for parts in range(1, FAR_PARTS + 1):
             fits = needed <= 1 if parts == 1 else needed == parts
 
@@ -346,7 +378,9 @@
             halo_copy(n, 1, -1).wait_send()
 
     for part in range(2):
-        for_each_target(part, lambda copy: copy.wait_send())
+        own_copies(part, lambda copy: copy.wait_send())
+        for d in range(1, chips):
+            passed_copies(part, d, lambda copy: copy.wait_send())
 
 
 def attention(queries, pairs, query_taps, pair_taps, out_gain, shards):
@@ -381,12 +415,8 @@
             dma((2,)),
             dma((2, 2)),
             dma((2, 2)),
-            dma((shards,)),
-            dma((shards,)),
-            dma((2 * shards,)),
-            dma((shards,)),
-            dma((shards,)),
-            dma((2 * shards,)),
+            dma((2, 2, shards)),
+            dma((2, 2 * shards)),
             dma((blocks,)),
         ],
         compiler_params=pltpu.CompilerParams(

time: 19.3 us -> 18.3 us (0.948)
  Pallas kernels: 16.9 us -> 15.8 us
    pallas_call x1, Pallas kernels: 16.9 us -> 15.8 us  [attention(): pl.pallas_call(functools.partial(kernel, shards, per_span, heads), out_sh...]
where the time goes in v3:
time: 18.3 us; the launch traced here: 18.1 us
  Pallas kernels  15.8 us (86%)
  local copies, waits for them, and re-layouts  2.26 us (12%)
    pallas_call x1, Pallas kernels, attention(): pl.pallas_call(functools.partial(kernel, shards, per_span, heads), out_sh...  15.8 us
    unnamed x1, local copies, waits for them, and re-layouts  2.26 us

profile of v3, /device:TPU:0, one launch (start us, length us, event | category | flops | bytes accessed | tf_op | source)
XLA Modules:
  0.0 18.1 jit_solution(11874545010614124208)
XLA Ops:
  0.0 15.8 %conv_attention.1 = bf16[1024,512]{1,0:T(8,128)(2,1)} custom-call(bf16[1024,512]{1,0:T(8,128)(2,1)} %q_hbm.1, bf16[1024,256]{1,0:T(8,128)(2,1)} %kv_hbm.1, f32[4,512]{1,0:T(4,128)} %qt_hbm.1, f32[4,256]{1,0:T(4,128)} %pt_hbm.1, f32[1,512]{1,0:T(1,128)} %bitcast.1, bf16[16,128]{1,0:T(8,128)(2,1)} %constant.2.clone.table_hbm), custom_call_target="tpu_custom_call" | custom-call | tf_op jit(solution)/shard_map/conv_attention/pallas_call | solution.py:397
  15.8 2.3 %copy.8 = bf16[1024,512]{1,0:T(8,128)(2,1)} copy(bf16[1024,512]{1,0:T(8,128)(2,1)} %conv_attention.1) | data formatting | bytes 2097152

commit v4 on v3

--- a/solution.py
+++ b/solution.py
@@ -36,6 +36,72 @@
     return lax.dot_general(
         left, right, (((1,), (1,)), ((), ())), preferred_element_type=jnp.float32
     )
+
+
+def loop(low, high, body):
+    def step(i, carry):
+        body(i)
+        return carry
+
+    lax.fori_loop(low, high, step, 0)
+
+
+def block_of(place, shards, per_span, index):
+    upper = index // per_span
+    span = place + upper * (2 * shards - 1 - 2 * place)
+    return span * per_span + lax.rem(index, per_span)
+
+
+def attend_block(qc, kvc, gath, gain, out, index, block_id, part_rows, least, most):
+    needed = (block_id * KEEP + part_rows - 1) // part_rows
+    for parts in range(least, most + 1):
+        fits = needed <= least if parts == least else needed == parts
+
+        @pl.when(fits)
+        def _():
+            attend(qc, kvc, gath, gain, out, index, block_id, part_rows, parts)
+
+
+def attend(qc, kvc, gath, gain, out, index, block_id, part_rows, parts):
+    block, channels = TRANSFORM_BLOCK, HEAD_CHANNELS
+    heads, half = qc.shape[1], gath.shape[1]
+    scale = math.log2(math.e) / math.sqrt(channels)
+    row_id = lax.broadcasted_iota(jnp.int32, (block, block), 0)
+    column_id = lax.broadcasted_iota(jnp.int32, (block, block), 1)
+    far_rows = parts * part_rows
+    near = kvc[index]
+    far = gath[: far_rows // half].reshape(far_rows, 2 * channels)
+    near_bias = jnp.where(row_id >= column_id, 0.0, NEGATIVE)
+    far_ids = lax.broadcasted_iota(jnp.int32, (1, part_rows), 1)
+    far_bias = jnp.where(
+        far_ids + (far_rows - part_rows) < block_id * KEEP, 0.0, NEGATIVE
+    )
+    values = jnp.concatenate([near[:, channels:], far[:, channels:]], 0)
+    values = jnp.concatenate([values, jnp.ones_like(values)], 1)
+    rows = pl.ds(pl.multiple_of(index * block, block), block)
+    some = min(heads, 2)
+    for begin in range(0, heads, some):
+        query = qc[index, begin : begin + some].reshape(some * block, channels)
+        near_scores = nt_dot(query, near[:, :channels])
+        near_scores = (
+            near_scores.reshape(some, block, block) + near_bias[None]
+        ).reshape(some * block, block)
+        far_scores = nt_dot(query, far[:, :channels])
+        pieces = [near_scores, far_scores[:, far_rows - part_rows :] + far_bias]
+        if parts > 1:
+            pieces.insert(1, far_scores[:, : far_rows - part_rows])
+        scores = jnp.concatenate(pieces, 1)
+        top = jnp.max(scores, -1, keepdims=True)
+        weights = jnp.exp2((scores - top) * scale).astype(jnp.bfloat16)
+        both = jnp.dot(weights, values, preferred_element_type=jnp.float32)
+        summed, total = both[:, :channels], both[:, channels:]
+        mean = jnp.mean(summed * summed, -1, keepdims=True)
+        normed = summed * lax.rsqrt(mean + EPSILON * (total * total))
+        for h in range(some):
+            columns = pl.ds((begin + h) * channels, channels)
+            out[rows, columns] = (
+                normed[h * block : (h + 1) * block] * gain[:, columns]
+            ).astype(jnp.bfloat16)
 
 
 def kernel(
@@ -48,7 +114,10 @@
     pt_hbm,
     gahbm,
     table_hbm,
-    out_hbm,
+    low_hbm,
+    qc_hbm,
+    kvc_hbm,
+    gath_hbm,
     xq,
     xkv,
     qt,
@@ -67,6 +136,7 @@
     span_send,
     span_recv,
     out_sem,
+    hand_sem,
 ):
     place = lax.axis_index("ctx")
     block = TRANSFORM_BLOCK
@@ -197,13 +267,6 @@
         for h in range(heads):
             qc[s * per_span + i, h] = conv(xq, s, i, qt, h)
 
-    def loop(low, high, body):
-        def step(i, carry):
-            body(i)
-            return carry
-
-        lax.fori_loop(low, high, step, 0)
-
     small[0].wait()
     small[1].wait()
     for s in range(2):
@@ -235,17 +298,25 @@
     def own_copies(part, act):
         for d in range(1, chips):
             target = peer(d)
+            other = target + 1 - 2 * lax.rem(target, 2)
             act(span_copy(0, spans[0], target, part, d))
+            when(
+                target > place,
+                lambda: act(span_copy(0, spans[0], other, part, shards + d)),
+            )
             when(target < place, lambda: act(span_copy(1, spans[1], target, part, d)))
         act(span_copy(0, spans[0], mate, part, 0))
         when(mate < place, lambda: act(span_copy(1, spans[1], mate, part, 0)))
 
     def passed_copies(part, d, act):
         source = peer(d)
-        hop = chips - 1 + d
-        act(span_copy(0, source, mate, part, hop))
         upper = 2 * shards - 1 - source
-        when(source > place, lambda: act(span_copy(1, upper, mate, part, hop)))
+
+        def both():
+            act(span_copy(0, source, mate, part, shards + chips + d))
+            act(span_copy(1, upper, mate, part, shards + chips + d))
+
+        when(source > place, both)
 
     def arrive(s, q, part):
         span = (q, 2 * shards - 1 - q)[s]
@@ -254,8 +325,12 @@
     def pass_on(part):
         for d in range(1, chips):
             source = peer(d)
-            arrive(0, source, part)
-            when(source > place, lambda: arrive(1, source, part))
+
+            def both():
+                arrive(0, source, part)
+                arrive(1, source, part)
+
+            when(source > place, both)
             passed_copies(part, d, lambda copy: copy.start())
 
     own_copies(1, lambda copy: copy.start())
@@ -273,64 +348,16 @@
     for s in range(2):
         query_block(s, 0)
 
-    scale = math.log2(math.e) / math.sqrt(channels)
-    row_id = lax.broadcasted_iota(jnp.int32, (block, block), 0)
-    column_id = lax.broadcasted_iota(jnp.int32, (block, block), 1)
-
+    block_id = functools.partial(block_of, place, shards, per_span)
     part_rows = 2 * shards * half // FAR_PARTS
 
-    def attend(index, parts):
-        far_rows = parts * part_rows
-        near = kvc[index]
-        far = gath[: far_rows // half].reshape(far_rows, 2 * channels)
-        near_bias = jnp.where(row_id >= column_id, 0.0, NEGATIVE)
-        far_ids = lax.broadcasted_iota(jnp.int32, (1, part_rows), 1)
-        far_bias = jnp.where(
-            far_ids + (far_rows - part_rows) < block_id(index) * KEEP, 0.0, NEGATIVE
-        )
-        values = jnp.concatenate([near[:, channels:], far[:, channels:]], 0)
-        values = jnp.concatenate([values, jnp.ones_like(values)], 1)
-        rows = pl.ds(pl.multiple_of(index * block, block), block)
-        some = min(heads, 2)
-        for begin in range(0, heads, some):
-            query = qc[index, begin : begin + some].reshape(some * block, channels)
-            near_scores = nt_dot(query, near[:, :channels])
-            near_scores = (
-                near_scores.reshape(some, block, block) + near_bias[None]
-            ).reshape(some * block, block)
-            far_scores = nt_dot(query, far[:, :channels])
-            pieces = [near_scores, far_scores[:, far_rows - part_rows :] + far_bias]
-            if parts > 1:
-                pieces.insert(1, far_scores[:, : far_rows - part_rows])
-            scores = jnp.concatenate(pieces, 1)
-            top = jnp.max(scores, -1, keepdims=True)
-            weights = jnp.exp2((scores - top) * scale).astype(jnp.bfloat16)
-            both = jnp.dot(weights, values, preferred_element_type=jnp.float32)
-            summed, total = both[:, :channels], both[:, channels:]
-            mean = jnp.mean(summed * summed, -1, keepdims=True)
-            normed = summed * lax.rsqrt(mean + EPSILON * (total * total))
-            for h in range(some):
-                columns = pl.ds((begin + h) * channels, channels)
-                out[rows, columns] = (
-                    normed[h * block : (h + 1) * block] * gain[:, columns]
-                ).astype(jnp.bfloat16)
-        out_copy(index).start()
-
-    def out_copy(index):
-        rows = pl.ds(pl.multiple_of(index * block, block), block)
-        return pltpu.make_async_copy(
-            out.at[rows, :], out_hbm.at[rows, :], out_sem.at[index]
-        )
-
-    def block_id(index):
-        upper = index // per_span
-        span = place + upper * (2 * shards - 1 - 2 * place)
-        return span * per_span + lax.rem(index, per_span)
-
-    def from_mate(s, q):
-        return jnp.logical_and(
-            lax.rem(q, 2) == lax.rem(mate, 2), (q >= 0) if s == 0 else (q > place)
-        )
+    def low_copy(i):
+        rows = pl.ds(pl.multiple_of(i * block, block), block)
+        return pltpu.make_async_copy(out.at[rows, :], low_hbm.at[rows, :], out_sem.at[i])
+
+    def awaited(s, q):
+        passed = jnp.logical_and(lax.rem(q, 2) == lax.rem(place, 2), q > place)
+        return jnp.logical_and(jnp.logical_not(passed), (q != place) if s == 0 else (q > place))
 
     def needed_parts(index):
         return (block_id(index) * KEEP + part_rows - 1) // part_rows
@@ -341,31 +368,54 @@
         for q in range(shards):
             wanted = jnp.logical_and(q >= low, q < high)
 
-            @pl.when(jnp.logical_and(wanted, from_mate(s, q)))
+            @pl.when(jnp.logical_and(wanted, awaited(s, q)))
             def _():
                 for part in range(2):
                     arrive(s, q, part)
 
-    pass_on(1)
-    pass_on(0)
+    handed = [
+        pltpu.make_async_copy(source, target, hand_sem.at[n])
+        for n, (source, target) in enumerate(
+            [
+                (qc.at[pl.ds(per_span, per_span)], qc_hbm),
+                (kvc.at[pl.ds(per_span, per_span)], kvc_hbm),
+                (gath, gath_hbm),
+            ]
+        )
+    ]
+    handed[0].start()
+    handed[1].start()
+
+    early = lower_spans > place - lax.rem(place, 2) + 2
+
+    @pl.when(early)
+    def _():
+        pass_on(1)
+        pass_on(0)
+
     await_spans(0, 0, lower_spans)
 
     def step(index):
-        @pl.when(index == per_span)
+        @pl.when(jnp.logical_and(index == min(1, per_span - 1), jnp.logical_not(early)))
+        def _():
+            pass_on(1)
+            pass_on(0)
+
+        @pl.when(index == per_span - 1)
         def _():
             await_spans(0, lower_spans, shards)
             await_spans(1, 0, shards)
-
-        needed = needed_parts(index)
-        for parts in range(1, FAR_PARTS + 1):
-            fits = needed <= 1 if parts == 1 else needed == parts
-
-            @pl.when(fits)
-            def _():
-                attend(index, parts)
-
-    loop(0, 2 * per_span, step)
-    loop(0, 2 * per_span, lambda index: out_copy(index).wait())
+            handed[2].start()
+
+        attend_block(
+            qc, kvc, gath, gain, out, index, block_id(index), part_rows, 1, FAR_PARTS // 2
+        )
+        low_copy(index).start()
+
+    loop(0, per_span, step)
+    loop(0, per_span, lambda index: low_copy(index).wait())
+    for copy in handed:
+        copy.wait()
 
     for n in range(2):
 
@@ -381,6 +431,73 @@
         own_copies(part, lambda copy: copy.wait_send())
         for d in range(1, chips):
             passed_copies(part, d, lambda copy: copy.wait_send())
+
+
+def upper_kernel(
+    shards,
+    per_span,
+    heads,
+    low_hbm,
+    qc_hbm,
+    kvc_hbm,
+    gath_hbm,
+    gain_hbm,
+    out_hbm,
+    qc,
+    kvc,
+    gath,
+    gain,
+    out,
+    in_sem,
+    q_sem,
+    out_sem,
+    low_sem,
+):
+    place = lax.axis_index("ctx")
+    block = TRANSFORM_BLOCK
+    span_rows = per_span * block
+    part_rows = 2 * shards * per_span * KEEP // FAR_PARTS
+
+    loads = [
+        pltpu.make_async_copy(source, target, in_sem.at[n])
+        for n, (source, target) in enumerate(
+            [(gath_hbm, gath), (kvc_hbm, kvc), (gain_hbm, gain)]
+        )
+    ]
+
+    def query_load(i):
+        return pltpu.make_async_copy(qc_hbm.at[i], qc.at[i], q_sem.at[i])
+
+    query_load(0).start()
+    for copy in loads:
+        copy.start()
+    loop(1, per_span, lambda i: query_load(i).start())
+    low_copy = pltpu.make_async_copy(
+        low_hbm, out_hbm.at[pl.ds(0, span_rows), :], low_sem
+    )
+    low_copy.start()
+
+    def out_copy(i):
+        rows = pl.ds(pl.multiple_of(i * block, block), block)
+        target = pl.ds(pl.multiple_of(span_rows + i * block, block), block)
+        return pltpu.make_async_copy(
+            out.at[rows, :], out_hbm.at[target, :], out_sem.at[i]
+        )
+
+    for copy in loads:
+        copy.wait()
+
+    def step(i):
+        query_load(i).wait()
+        block_id = block_of(place, shards, per_span, per_span + i)
+        attend_block(
+            qc, kvc, gath, gain, out, i, block_id, part_rows, FAR_PARTS // 2, FAR_PARTS
+        )
+        out_copy(i).start()
+
+    loop(0, per_span, step)
+    loop(0, per_span, lambda i: out_copy(i).wait())
+    low_copy.wait()
 
 
 def attention(queries, pairs, query_taps, pair_taps, out_gain, shards):
@@ -394,11 +511,20 @@
     width = 2 * HEAD_CHANNELS
     hbm = pl.BlockSpec(memory_space=pltpu.HBM)
     dma = pltpu.SemaphoreType.DMA
-    return pl.pallas_call(
+    gain = out_gain.reshape(1, columns)
+    half_q = (per_span, heads, TRANSFORM_BLOCK, HEAD_CHANNELS)
+    half_kv = (per_span, TRANSFORM_BLOCK, width)
+    all_packed = (2 * shards, half, width)
+    handed = pl.pallas_call(
         functools.partial(kernel, shards, per_span, heads),
-        out_shape=jax.ShapeDtypeStruct((rows, columns), bf16),
+        out_shape=[
+            jax.ShapeDtypeStruct((span_rows, columns), bf16),
+            jax.ShapeDtypeStruct(half_q, bf16),
+            jax.ShapeDtypeStruct(half_kv, bf16),
+            jax.ShapeDtypeStruct(all_packed, bf16),
+        ],
         in_specs=[hbm] * 6,
-        out_specs=hbm,
+        out_specs=[hbm] * 4,
         scratch_shapes=[
             pltpu.VMEM((2, HALO + span_rows, columns), bf16),
             pltpu.VMEM((2, HALO + span_rows, width), bf16),
@@ -408,29 +534,49 @@
             pltpu.VMEM((KEEP, TRANSFORM_BLOCK), bf16),
             pltpu.VMEM((blocks, heads, TRANSFORM_BLOCK, HEAD_CHANNELS), bf16),
             pltpu.VMEM((blocks, TRANSFORM_BLOCK, width), bf16),
-            pltpu.VMEM((2 * shards, half, width), bf16),
-            pltpu.VMEM((rows, columns), bf16),
+            pltpu.VMEM(all_packed, bf16),
+            pltpu.VMEM((span_rows, columns), bf16),
             dma((4,)),
             dma((4,)),
             dma((2,)),
             dma((2, 2)),
             dma((2, 2)),
-            dma((2, 2, shards)),
+            dma((2, 2, 2 * shards)),
             dma((2, 2 * shards)),
-            dma((blocks,)),
+            dma((per_span,)),
+            dma((3,)),
         ],
         compiler_params=pltpu.CompilerParams(
             collective_id=0, has_side_effects=True, vmem_limit_bytes=62 * 1024 * 1024
         ),
-        name="conv_attention",
+        name="exchange_and_lower",
     )(
         queries,
         pairs,
         query_taps,
         pair_taps,
-        out_gain.reshape(1, columns),
+        gain,
         jnp.asarray(dct_table()),
     )
+    return pl.pallas_call(
+        functools.partial(upper_kernel, shards, per_span, heads),
+        out_shape=jax.ShapeDtypeStruct((rows, columns), bf16),
+        in_specs=[hbm] * 5,
+        out_specs=hbm,
+        scratch_shapes=[
+            pltpu.VMEM(half_q, bf16),
+            pltpu.VMEM(half_kv, bf16),
+            pltpu.VMEM(all_packed, bf16),
+            pltpu.VMEM((1, columns), f32),
+            pltpu.VMEM((span_rows, columns), bf16),
+            dma((3,)),
+            dma((per_span,)),
+            dma((per_span,)),
+            dma,
+        ],
+        compiler_params=pltpu.CompilerParams(vmem_limit_bytes=62 * 1024 * 1024),
+        name="upper",
+    )(*handed, gain)
 
 
 def from_partner(block, axis, apart):

time: 18.3 us -> 28.9 us (1.58)
  Pallas kernels: 15.8 us -> 28.7 us
  local copies, waits for them, and re-layouts: 2.26 us -> 0 us
    pallas_call x0 -> x1, Pallas kernels: none -> 17.1 us  [attention(): pl.pallas_call(functools.partial(upper_kernel, shards, per_span, heads),...]
    pallas_call x1, Pallas kernels: 15.8 us -> 11.6 us  [attention(): pl.pallas_call(functools.partial(kernel, shards, per_span, heads), out_sh...]
    unnamed x1 -> x0, local copies, waits for them, and re-layouts: 2.26 us -> none
where the time goes in v4:
time: 28.9 us; the launch traced here: 28.8 us
  Pallas kernels  28.7 us (99%)
    pallas_call x1, Pallas kernels, attention(): pl.pallas_call(functools.partial(upper_kernel, shards, per_span, heads),...  17.1 us
    pallas_call x1, Pallas kernels, attention(): pl.pallas_call(functools.partial(kernel, shards, per_span, heads), out_sh...  11.6 us

profile of v4, /device:TPU:0, one launch (start us, length us, event | category | flops | bytes accessed | tf_op | source)
XLA Modules:
  0.0 28.8 jit_solution(6169863843792021202)
XLA Ops:
  0.0 11.6 %exchange_and_lower.1 = (bf16[512,512]{1,0:T(8,128)(2,1)}, bf16[4,4,128,128]{3,2,1,0:T(8,128)(2,1)}, bf16[4,128,256]{2,1,0:T(8,128)(2,1)}, bf16[8,64,256]{2,1,0:T(8,128)(2,1)}) custom-call(bf16[1024,512]{1,0:T(8,128)(2,1)} %q_hbm.1, bf16[1024,256]{1,0:T(8,128)(2,1)} %kv_hbm.1, f32[4,512]{1,0:T(4,128)} %qt_hbm.1, f32[4,256]{1,0:T(4,128)} %pt_hbm.1, ...), custom_call_target="tpu_custom_call" | custom-call | tf_op jit(solution)/shard_map/exchange_and_lower/pallas_call | solution.py:518
  11.6 17.1 %upper.1 = bf16[1024,512]{1,0:T(8,128)(2,1)} custom-call(bf16[512,512]{1,0:T(8,128)(2,1)} %get-tuple-element.9.low_hbm, bf16[4,4,128,128]{3,2,1,0:T(8,128)(2,1)} %get-tuple-element.10.qc_hbm, bf16[4,128,256]{2,1,0:T(8,128)(2,1)} %get-tuple-element.11.kvc_hbm, bf16[8,64,256]{2,1,0:T(8,128)(2,1)} %get-tuple-element.12.gath_hbm, f32[1,512]{1,0:T(1,128)} %bitcast.2), custom_call_target="tpu_custom_call" | custom-call | tf_op jit(solution)/shard_map/upper/pallas_call | solution.py:561

commit v5 on v4

--- a/solution.py
+++ b/solution.py
@@ -448,6 +448,7 @@
     gath,
     gain,
     out,
+    low,
     in_sem,
     q_sem,
     out_sem,
@@ -472,10 +473,11 @@
     for copy in loads:
         copy.start()
     loop(1, per_span, lambda i: query_load(i).start())
-    low_copy = pltpu.make_async_copy(
-        low_hbm, out_hbm.at[pl.ds(0, span_rows), :], low_sem
+    low_load = pltpu.make_async_copy(low_hbm, low, low_sem.at[0])
+    low_store = pltpu.make_async_copy(
+        low, out_hbm.at[pl.ds(0, span_rows), :], low_sem.at[1]
     )
-    low_copy.start()
+    low_load.start()
 
     def out_copy(i):
         rows = pl.ds(pl.multiple_of(i * block, block), block)
@@ -495,9 +497,14 @@
         )
         out_copy(i).start()
 
+        @pl.when(i == 0)
+        def _():
+            low_load.wait()
+            low_store.start()
+
     loop(0, per_span, step)
     loop(0, per_span, lambda i: out_copy(i).wait())
-    low_copy.wait()
+    low_store.wait()
 
 
 def attention(queries, pairs, query_taps, pair_taps, out_gain, shards):
@@ -569,10 +576,11 @@
             pltpu.VMEM(all_packed, bf16),
             pltpu.VMEM((1, columns), f32),
             pltpu.VMEM((span_rows, columns), bf16),
+            pltpu.VMEM((span_rows, columns), bf16),
             dma((3,)),
             dma((per_span,)),
             dma((per_span,)),
-            dma,
+            dma((2,)),
         ],
         compiler_params=pltpu.CompilerParams(vmem_limit_bytes=62 * 1024 * 1024),
         name="upper",

time: 28.9 us -> 17.4 us (0.60)
  the two profiles are of different devices: /device:TPU:0 before, /device:TPU:11 now
where the time goes in v5:
time: 17.4 us; the launch traced here: 17.3 us
  Pallas kernels  17.3 us (99%)
    pallas_call x1, Pallas kernels, attention(): pl.pallas_call(functools.partial(kernel, shards, per_span, heads), out_sh...  11.3 us
    pallas_call x1, Pallas kernels, attention(): pl.pallas_call(functools.partial(upper_kernel, shards, per_span, heads),...  6 us

profile of v5, /device:TPU:11, one launch (start us, length us, event | category | flops | bytes accessed | tf_op | source)
XLA Modules:
  0.0 17.3 jit_solution(17924895990353745529)
XLA Ops:
  0.0 11.3 %exchange_and_lower.1 = (bf16[512,512]{1,0:T(8,128)(2,1)}, bf16[4,4,128,128]{3,2,1,0:T(8,128)(2,1)}, bf16[4,128,256]{2,1,0:T(8,128)(2,1)}, bf16[8,64,256]{2,1,0:T(8,128)(2,1)}) custom-call(bf16[1024,512]{1,0:T(8,128)(2,1)} %q_hbm.1, bf16[1024,256]{1,0:T(8,128)(2,1)} %kv_hbm.1, f32[4,512]{1,0:T(4,128)} %qt_hbm.1, f32[4,256]{1,0:T(4,128)} %pt_hbm.1, ...), custom_call_target="tpu_custom_call" | custom-call | tf_op jit(solution)/shard_map/exchange_and_lower/pallas_call | solution.py:525
  11.3 6.0 %upper.1 = bf16[1024,512]{1,0:T(8,128)(2,1)} custom-call(bf16[512,512]{1,0:T(8,128)(2,1)} %get-tuple-element.9.low_hbm, bf16[4,4,128,128]{3,2,1,0:T(8,128)(2,1)} %get-tuple-element.10.qc_hbm, bf16[4,128,256]{2,1,0:T(8,128)(2,1)} %get-tuple-element.11.kvc_hbm, bf16[8,64,256]{2,1,0:T(8,128)(2,1)} %get-tuple-element.12.gath_hbm, f32[1,512]{1,0:T(1,128)} %bitcast.2), custom_call_target="tpu_custom_call" | custom-call | tf_op jit(solution)/shard_map/upper/pallas_call | solution.py:568

commit v6 on v5

--- a/solution.py
+++ b/solution.py
@@ -76,20 +76,20 @@
     far_bias = jnp.where(
         far_ids + (far_rows - part_rows) < block_id * KEEP, 0.0, NEGATIVE
     )
+    keys = jnp.concatenate([near[:, :channels], far[:, :channels]], 0)
     values = jnp.concatenate([near[:, channels:], far[:, channels:]], 0)
     values = jnp.concatenate([values, jnp.ones_like(values)], 1)
     rows = pl.ds(pl.multiple_of(index * block, block), block)
-    some = min(heads, 2)
+    some = heads
     for begin in range(0, heads, some):
         query = qc[index, begin : begin + some].reshape(some * block, channels)
-        near_scores = nt_dot(query, near[:, :channels])
+        scores = nt_dot(query, keys)
         near_scores = (
-            near_scores.reshape(some, block, block) + near_bias[None]
+            scores[:, :block].reshape(some, block, block) + near_bias[None]
         ).reshape(some * block, block)
-        far_scores = nt_dot(query, far[:, :channels])
-        pieces = [near_scores, far_scores[:, far_rows - part_rows :] + far_bias]
+        pieces = [near_scores, scores[:, block + far_rows - part_rows :] + far_bias]
         if parts > 1:
-            pieces.insert(1, far_scores[:, : far_rows - part_rows])
+            pieces.insert(1, scores[:, block : block + far_rows - part_rows])
         scores = jnp.concatenate(pieces, 1)
         top = jnp.max(scores, -1, keepdims=True)
         weights = jnp.exp2((scores - top) * scale).astype(jnp.bfloat16)

time: 17.4 us -> 18.2 us (1.046)
  the two profiles are of different devices: /device:TPU:11 before, /device:TPU:0 now
where the time goes in v6:
time: 18.2 us; the launch traced here: 18.1 us
  Pallas kernels  18.1 us (99%)
    pallas_call x1, Pallas kernels, attention(): pl.pallas_call(functools.partial(kernel, shards, per_span, heads), out_sh...  11.5 us
    pallas_call x1, Pallas kernels, attention(): pl.pallas_call(functools.partial(upper_kernel, shards, per_span, heads),...  6.53 us

profile of v6, /device:TPU:0, one launch (start us, length us, event | category | flops | bytes accessed | tf_op | source)
XLA Modules:
  0.0 18.1 jit_solution(5890977212817786771)
XLA Ops:
  0.0 11.5 %exchange_and_lower.1 = (bf16[512,512]{1,0:T(8,128)(2,1)}, bf16[4,4,128,128]{3,2,1,0:T(8,128)(2,1)}, bf16[4,128,256]{2,1,0:T(8,128)(2,1)}, bf16[8,64,256]{2,1,0:T(8,128)(2,1)}) custom-call(bf16[1024,512]{1,0:T(8,128)(2,1)} %q_hbm.1, bf16[1024,256]{1,0:T(8,128)(2,1)} %kv_hbm.1, f32[4,512]{1,0:T(4,128)} %qt_hbm.1, f32[4,256]{1,0:T(4,128)} %pt_hbm.1, ...), custom_call_target="tpu_custom_call" | custom-call | tf_op jit(solution)/shard_map/exchange_and_lower/pallas_call | solution.py:525
  11.5 6.5 %upper.1 = bf16[1024,512]{1,0:T(8,128)(2,1)} custom-call(bf16[512,512]{1,0:T(8,128)(2,1)} %get-tuple-element.9.low_hbm, bf16[4,4,128,128]{3,2,1,0:T(8,128)(2,1)} %get-tuple-element.10.qc_hbm, bf16[4,128,256]{2,1,0:T(8,128)(2,1)} %get-tuple-element.11.kvc_hbm, bf16[8,64,256]{2,1,0:T(8,128)(2,1)} %get-tuple-element.12.gath_hbm, f32[1,512]{1,0:T(1,128)} %bitcast.2), custom_call_target="tpu_custom_call" | custom-call | tf_op jit(solution)/shard_map/upper/pallas_call | solution.py:568

commit v7 on v5

--- a/solution.py
+++ b/solution.py
@@ -52,56 +52,56 @@
     return span * per_span + lax.rem(index, per_span)
 
 
-def attend_block(qc, kvc, gath, gain, out, index, block_id, part_rows, least, most):
-    needed = (block_id * KEEP + part_rows - 1) // part_rows
+def attend_blocks(qc, kvc, gath, gain, out, index, count, block_id, part_rows, least, most):
+    needed = ((block_id + count - 1) * KEEP + part_rows - 1) // part_rows
     for parts in range(least, most + 1):
         fits = needed <= least if parts == least else needed == parts
 
         @pl.when(fits)
         def _():
-            attend(qc, kvc, gath, gain, out, index, block_id, part_rows, parts)
-
-
-def attend(qc, kvc, gath, gain, out, index, block_id, part_rows, parts):
+            attend(qc, kvc, gath, gain, out, index, count, block_id, part_rows, parts)
+
+
+def attend(qc, kvc, gath, gain, out, index, count, block_id, part_rows, parts):
     block, channels = TRANSFORM_BLOCK, HEAD_CHANNELS
     heads, half = qc.shape[1], gath.shape[1]
     scale = math.log2(math.e) / math.sqrt(channels)
     row_id = lax.broadcasted_iota(jnp.int32, (block, block), 0)
     column_id = lax.broadcasted_iota(jnp.int32, (block, block), 1)
+    near_bias = jnp.where(row_id >= column_id, 0.0, NEGATIVE)
     far_rows = parts * part_rows
-    near = kvc[index]
+    open_rows = block + far_rows - part_rows
     far = gath[: far_rows // half].reshape(far_rows, 2 * channels)
-    near_bias = jnp.where(row_id >= column_id, 0.0, NEGATIVE)
-    far_ids = lax.broadcasted_iota(jnp.int32, (1, part_rows), 1)
-    far_bias = jnp.where(
-        far_ids + (far_rows - part_rows) < block_id * KEEP, 0.0, NEGATIVE
-    )
-    values = jnp.concatenate([near[:, channels:], far[:, channels:]], 0)
-    values = jnp.concatenate([values, jnp.ones_like(values)], 1)
-    rows = pl.ds(pl.multiple_of(index * block, block), block)
+    far_ids = lax.broadcasted_iota(jnp.int32, (1, part_rows), 1) + (far_rows - part_rows)
     some = min(heads, 2)
-    for begin in range(0, heads, some):
-        query = qc[index, begin : begin + some].reshape(some * block, channels)
-        near_scores = nt_dot(query, near[:, :channels])
-        near_scores = (
-            near_scores.reshape(some, block, block) + near_bias[None]
-        ).reshape(some * block, block)
-        far_scores = nt_dot(query, far[:, :channels])
-        pieces = [near_scores, far_scores[:, far_rows - part_rows :] + far_bias]
-        if parts > 1:
-            pieces.insert(1, far_scores[:, : far_rows - part_rows])
-        scores = jnp.concatenate(pieces, 1)
-        top = jnp.max(scores, -1, keepdims=True)
-        weights = jnp.exp2((scores - top) * scale).astype(jnp.bfloat16)
-        both = jnp.dot(weights, values, preferred_element_type=jnp.float32)
-        summed, total = both[:, :channels], both[:, channels:]
-        mean = jnp.mean(summed * summed, -1, keepdims=True)
-        normed = summed * lax.rsqrt(mean + EPSILON * (total * total))
-        for h in range(some):
-            columns = pl.ds((begin + h) * channels, channels)
-            out[rows, columns] = (
-                normed[h * block : (h + 1) * block] * gain[:, columns]
-            ).astype(jnp.bfloat16)
+    for step in range(count):
+        near = kvc[index + step]
+        far_bias = jnp.where(far_ids < (block_id + step) * KEEP, 0.0, NEGATIVE)
+        keys = jnp.concatenate([near[:, :channels], far[:, :channels]], 0)
+        values = jnp.concatenate([near[:, channels:], far[:, channels:]], 0)
+        values = jnp.concatenate([values, jnp.ones_like(values)], 1)
+        rows = pl.ds(pl.multiple_of((index + step) * block, block), block)
+        for begin in range(0, heads, some):
+            query = qc[index + step, begin : begin + some].reshape(some * block, channels)
+            scores = nt_dot(query, keys)
+            near_scores = (
+                scores[:, :block].reshape(some, block, block) + near_bias[None]
+            ).reshape(some * block, block)
+            pieces = [near_scores, scores[:, open_rows:] + far_bias]
+            if parts > 1:
+                pieces.insert(1, scores[:, block:open_rows])
+            scores = jnp.concatenate(pieces, 1)
+            top = jnp.max(scores, -1, keepdims=True)
+            weights = jnp.exp2((scores - top) * scale).astype(jnp.bfloat16)
+            both = jnp.dot(weights, values, preferred_element_type=jnp.float32)
+            summed, total = both[:, :channels], both[:, channels:]
+            mean = jnp.mean(summed * summed, -1, keepdims=True)
+            normed = summed * lax.rsqrt(mean + EPSILON * (total * total))
+            for h in range(some):
+                columns = pl.ds((begin + h) * channels, channels)
+                out[rows, columns] = (
+                    normed[h * block : (h + 1) * block] * gain[:, columns]
+                ).astype(jnp.bfloat16)
 
 
 def kernel(
@@ -334,16 +334,17 @@
             passed_copies(part, d, lambda copy: copy.start())
 
     own_copies(1, lambda copy: copy.start())
+    small[2].wait()
+    small[3].wait()
+    loads["q", 0].wait()
+    loop(1, per_span, functools.partial(query_block, 0))
     wait_halo(0)
     for s in range(2):
         pair_block(s, 0)
     own_copies(0, lambda copy: copy.start())
 
-    small[2].wait()
-    small[3].wait()
-    for s in range(2):
-        loads["q", s].wait()
-        loop(1, per_span, functools.partial(query_block, s))
+    loads["q", 1].wait()
+    loop(1, per_span, functools.partial(query_block, 1))
     wait_halo(1)
     for s in range(2):
         query_block(s, 0)
@@ -407,8 +408,8 @@
             await_spans(1, 0, shards)
             handed[2].start()
 
-        attend_block(
-            qc, kvc, gath, gain, out, index, block_id(index), part_rows, 1, FAR_PARTS // 2
+        attend_blocks(
+            qc, kvc, gath, gain, out, index, 1, block_id(index), part_rows, 1, FAR_PARTS // 2
         )
         low_copy(index).start()
 
@@ -489,20 +490,26 @@
     for copy in loads:
         copy.wait()
 
-    def step(i):
-        query_load(i).wait()
+    count = 2 - per_span % 2
+
+    def step(n):
+        i = n * count
+        for k in range(count):
+            query_load(i + k).wait()
         block_id = block_of(place, shards, per_span, per_span + i)
-        attend_block(
-            qc, kvc, gath, gain, out, i, block_id, part_rows, FAR_PARTS // 2, FAR_PARTS
-        )
-        out_copy(i).start()
-
-        @pl.when(i == 0)
+        least = FAR_PARTS // 2
+        attend_blocks(
+            qc, kvc, gath, gain, out, i, count, block_id, part_rows, least, FAR_PARTS
+        )
+        for k in range(count):
+            out_copy(i + k).start()
+
+        @pl.when(n == 0)
         def _():
             low_load.wait()
             low_store.start()
 
-    loop(0, per_span, step)
+    loop(0, per_span // count, step)
     loop(0, per_span, lambda i: out_copy(i).wait())
     low_store.wait()
 

time: 17.4 us -> 16.8 us (0.966)
  the two profiles are of different devices: /device:TPU:11 before, /device:TPU:0 now
where the time goes in v7:
time: 16.8 us; the launch traced here: 16.7 us
  Pallas kernels  16.6 us (99%)
    pallas_call x1, Pallas kernels, attention(): pl.pallas_call(functools.partial(kernel, shards, per_span, heads), out_sh...  11.5 us
    pallas_call x1, Pallas kernels, attention(): pl.pallas_call(functools.partial(upper_kernel, shards, per_span, heads),...  5.12 us

profile of v7, /device:TPU:0, one launch (start us, length us, event | category | flops | bytes accessed | tf_op | source)
XLA Modules:
  0.0 16.7 jit_solution(16849469162436197876)
XLA Ops:
  0.0 11.5 %exchange_and_lower.1 = (bf16[512,512]{1,0:T(8,128)(2,1)}, bf16[4,4,128,128]{3,2,1,0:T(8,128)(2,1)}, bf16[4,128,256]{2,1,0:T(8,128)(2,1)}, bf16[8,64,256]{2,1,0:T(8,128)(2,1)}) custom-call(bf16[1024,512]{1,0:T(8,128)(2,1)} %q_hbm.1, bf16[1024,256]{1,0:T(8,128)(2,1)} %kv_hbm.1, f32[4,512]{1,0:T(4,128)} %qt_hbm.1, f32[4,256]{1,0:T(4,128)} %pt_hbm.1, ...), custom_call_target="tpu_custom_call" | custom-call | tf_op jit(solution)/shard_map/exchange_and_lower/pallas_call | solution.py:532
  11.5 5.1 %upper.1 = bf16[1024,512]{1,0:T(8,128)(2,1)} custom-call(bf16[512,512]{1,0:T(8,128)(2,1)} %get-tuple-element.9.low_hbm, bf16[4,4,128,128]{3,2,1,0:T(8,128)(2,1)} %get-tuple-element.10.qc_hbm, bf16[4,128,256]{2,1,0:T(8,128)(2,1)} %get-tuple-element.11.kvc_hbm, bf16[8,64,256]{2,1,0:T(8,128)(2,1)} %get-tuple-element.12.gath_hbm, f32[1,512]{1,0:T(1,128)} %bitcast.2), custom_call_target="tpu_custom_call" | custom-call | tf_op jit(solution)/shard_map/upper/pallas_call | solution.py:575

commit v8 on v7

--- a/solution.py
+++ b/solution.py
@@ -32,12 +32,6 @@
     return table.astype(jnp.bfloat16)
 
 
-def nt_dot(left, right):
-    return lax.dot_general(
-        left, right, (((1,), (1,)), ((), ())), preferred_element_type=jnp.float32
-    )
-
-
 def loop(low, high, body):
     def step(i, carry):
         body(i)
@@ -52,17 +46,19 @@
     return span * per_span + lax.rem(index, per_span)
 
 
-def attend_blocks(qc, kvc, gath, gain, out, index, count, block_id, part_rows, least, most):
+def attend_blocks(qc, kvc, gath, turned, gain, out, index, count, block_id, part_rows, least, most):
     needed = ((block_id + count - 1) * KEEP + part_rows - 1) // part_rows
     for parts in range(least, most + 1):
         fits = needed <= least if parts == least else needed == parts
 
         @pl.when(fits)
         def _():
-            attend(qc, kvc, gath, gain, out, index, count, block_id, part_rows, parts)
-
-
-def attend(qc, kvc, gath, gain, out, index, count, block_id, part_rows, parts):
+            attend(
+                qc, kvc, gath, turned, gain, out, index, count, block_id, part_rows, parts
+            )
+
+
+def attend(qc, kvc, gath, turned, gain, out, index, count, block_id, part_rows, parts):
     block, channels = TRANSFORM_BLOCK, HEAD_CHANNELS
     heads, half = qc.shape[1], gath.shape[1]
     scale = math.log2(math.e) / math.sqrt(channels)
@@ -73,17 +69,18 @@
     open_rows = block + far_rows - part_rows
     far = gath[: far_rows // half].reshape(far_rows, 2 * channels)
     far_ids = lax.broadcasted_iota(jnp.int32, (1, part_rows), 1) + (far_rows - part_rows)
+    far_keys = far[:, :channels].T if turned is None else turned[:, :far_rows]
     some = min(heads, 2)
     for step in range(count):
         near = kvc[index + step]
         far_bias = jnp.where(far_ids < (block_id + step) * KEEP, 0.0, NEGATIVE)
-        keys = jnp.concatenate([near[:, :channels], far[:, :channels]], 0)
+        keys = jnp.concatenate([near[:, :channels].T, far_keys], 1)
         values = jnp.concatenate([near[:, channels:], far[:, channels:]], 0)
         values = jnp.concatenate([values, jnp.ones_like(values)], 1)
         rows = pl.ds(pl.multiple_of((index + step) * block, block), block)
         for begin in range(0, heads, some):
             query = qc[index + step, begin : begin + some].reshape(some * block, channels)
-            scores = nt_dot(query, keys)
+            scores = jnp.dot(query, keys, preferred_element_type=jnp.float32)
             near_scores = (
                 scores[:, :block].reshape(some, block, block) + near_bias[None]
             ).reshape(some * block, block)
@@ -345,6 +342,7 @@
 
     loads["q", 1].wait()
     loop(1, per_span, functools.partial(query_block, 1))
+    pass_on(1)
     wait_halo(1)
     for s in range(2):
         query_block(s, 0)
@@ -387,33 +385,28 @@
     handed[0].start()
     handed[1].start()
 
-    early = lower_spans > place - lax.rem(place, 2) + 2
-
-    @pl.when(early)
-    def _():
-        pass_on(1)
-        pass_on(0)
-
+    pass_on(0)
     await_spans(0, 0, lower_spans)
 
-    def step(index):
-        @pl.when(jnp.logical_and(index == min(1, per_span - 1), jnp.logical_not(early)))
-        def _():
-            pass_on(1)
-            pass_on(0)
-
-        @pl.when(index == per_span - 1)
+    count = 2 - per_span % 2
+
+    def step(n):
+        index = n * count
+
+        @pl.when(n == per_span // count - 1)
         def _():
             await_spans(0, lower_spans, shards)
             await_spans(1, 0, shards)
             handed[2].start()
 
+        most = FAR_PARTS // 2
         attend_blocks(
-            qc, kvc, gath, gain, out, index, 1, block_id(index), part_rows, 1, FAR_PARTS // 2
-        )
-        low_copy(index).start()
-
-    loop(0, per_span, step)
+            qc, kvc, gath, None, gain, out, index, count, block_id(index), part_rows, 1, most
+        )
+        for k in range(count):
+            low_copy(index + k).start()
+
+    loop(0, per_span // count, step)
     loop(0, per_span, lambda index: low_copy(index).wait())
     for copy in handed:
         copy.wait()
@@ -450,6 +443,7 @@
     gain,
     out,
     low,
+    turned,
     in_sem,
     q_sem,
     out_sem,
@@ -489,6 +483,7 @@
 
     for copy in loads:
         copy.wait()
+    turned[...] = gath[...].reshape(turned.shape[1], -1)[:, :HEAD_CHANNELS].T
 
     count = 2 - per_span % 2
 
@@ -499,7 +494,7 @@
         block_id = block_of(place, shards, per_span, per_span + i)
         least = FAR_PARTS // 2
         attend_blocks(
-            qc, kvc, gath, gain, out, i, count, block_id, part_rows, least, FAR_PARTS
+            qc, kvc, gath, turned, gain, out, i, count, block_id, part_rows, least, FAR_PARTS
         )
         for k in range(count):
             out_copy(i + k).start()
@@ -584,6 +579,7 @@
             pltpu.VMEM((1, columns), f32),
             pltpu.VMEM((span_rows, columns), bf16),
             pltpu.VMEM((span_rows, columns), bf16),
+            pltpu.VMEM((HEAD_CHANNELS, 2 * shards * half), bf16),
             dma((3,)),
             dma((per_span,)),
             dma((per_span,)),

time: 16.8 us -> 16.7 us (level)
    pallas_call x1, Pallas kernels: 11.5 us -> 11.3 us  [attention(): pl.pallas_call(functools.partial(kernel, shards, per_span, heads), out_sh...]
where the time goes in v8:
time: 16.7 us; the launch traced here: 16.5 us
  Pallas kernels  16.5 us (99%)
    pallas_call x1, Pallas kernels, attention(): pl.pallas_call(functools.partial(kernel, shards, per_span, heads), out_sh...  11.3 us
    pallas_call x1, Pallas kernels, attention(): pl.pallas_call(functools.partial(upper_kernel, shards, per_span, heads),...  5.26 us

profile of v8, /device:TPU:0, one launch (start us, length us, event | category | flops | bytes accessed | tf_op | source)
XLA Modules:
  0.0 16.5 jit_solution(5044110433514176305)
XLA Ops:
  0.0 11.3 %exchange_and_lower.1 = (bf16[512,512]{1,0:T(8,128)(2,1)}, bf16[4,4,128,128]{3,2,1,0:T(8,128)(2,1)}, bf16[4,128,256]{2,1,0:T(8,128)(2,1)}, bf16[8,64,256]{2,1,0:T(8,128)(2,1)}) custom-call(bf16[1024,512]{1,0:T(8,128)(2,1)} %q_hbm.1, bf16[1024,256]{1,0:T(8,128)(2,1)} %kv_hbm.1, f32[4,512]{1,0:T(4,128)} %qt_hbm.1, f32[4,256]{1,0:T(4,128)} %pt_hbm.1, ...), custom_call_target="tpu_custom_call" | custom-call | tf_op jit(solution)/shard_map/exchange_and_lower/pallas_call | solution.py:527
  11.3 5.3 %upper.1 = bf16[1024,512]{1,0:T(8,128)(2,1)} custom-call(bf16[512,512]{1,0:T(8,128)(2,1)} %get-tuple-element.9.low_hbm, bf16[4,4,128,128]{3,2,1,0:T(8,128)(2,1)} %get-tuple-element.10.qc_hbm, bf16[4,128,256]{2,1,0:T(8,128)(2,1)} %get-tuple-element.11.kvc_hbm, bf16[8,64,256]{2,1,0:T(8,128)(2,1)} %get-tuple-element.12.gath_hbm, f32[1,512]{1,0:T(1,128)} %bitcast.2), custom_call_target="tpu_custom_call" | custom-call | tf_op jit(solution)/shard_map/upper/pallas_call | solution.py:570

commit v9 on v8

--- a/solution.py
+++ b/solution.py
@@ -32,6 +32,12 @@
     return table.astype(jnp.bfloat16)
 
 
+def nt_dot(left, right):
+    return lax.dot_general(
+        left, right, (((1,), (1,)), ((), ())), preferred_element_type=jnp.float32
+    )
+
+
 def loop(low, high, body):
     def step(i, carry):
         body(i)
@@ -46,7 +52,7 @@
     return span * per_span + lax.rem(index, per_span)
 
 
-def attend_blocks(qc, kvc, gath, turned, gain, out, index, count, block_id, part_rows, least, most):
+def attend_blocks(qc, kvc, gath, gain, out, index, count, block_id, part_rows, least, most):
     needed = ((block_id + count - 1) * KEEP + part_rows - 1) // part_rows
     for parts in range(least, most + 1):
         fits = needed <= least if parts == least else needed == parts
@@ -54,11 +60,11 @@
         @pl.when(fits)
         def _():
             attend(
-                qc, kvc, gath, turned, gain, out, index, count, block_id, part_rows, parts
+                qc, kvc, gath, gain, out, index, count, block_id, part_rows, parts
             )
 
 
-def attend(qc, kvc, gath, turned, gain, out, index, count, block_id, part_rows, parts):
+def attend(qc, kvc, gath, gain, out, index, count, block_id, part_rows, parts):
     block, channels = TRANSFORM_BLOCK, HEAD_CHANNELS
     heads, half = qc.shape[1], gath.shape[1]
     scale = math.log2(math.e) / math.sqrt(channels)
@@ -69,18 +75,17 @@
     open_rows = block + far_rows - part_rows
     far = gath[: far_rows // half].reshape(far_rows, 2 * channels)
     far_ids = lax.broadcasted_iota(jnp.int32, (1, part_rows), 1) + (far_rows - part_rows)
-    far_keys = far[:, :channels].T if turned is None else turned[:, :far_rows]
     some = min(heads, 2)
     for step in range(count):
         near = kvc[index + step]
         far_bias = jnp.where(far_ids < (block_id + step) * KEEP, 0.0, NEGATIVE)
-        keys = jnp.concatenate([near[:, :channels].T, far_keys], 1)
+        keys = jnp.concatenate([near[:, :channels], far[:, :channels]], 0)
         values = jnp.concatenate([near[:, channels:], far[:, channels:]], 0)
         values = jnp.concatenate([values, jnp.ones_like(values)], 1)
         rows = pl.ds(pl.multiple_of((index + step) * block, block), block)
         for begin in range(0, heads, some):
             query = qc[index + step, begin : begin + some].reshape(some * block, channels)
-            scores = jnp.dot(query, keys, preferred_element_type=jnp.float32)
+            scores = nt_dot(query, keys)
             near_scores = (
                 scores[:, :block].reshape(some, block, block) + near_bias[None]
             ).reshape(some * block, block)
@@ -298,10 +303,15 @@
             other = target + 1 - 2 * lax.rem(target, 2)
             act(span_copy(0, spans[0], target, part, d))
             when(
-                target > place,
+                jnp.logical_or(target > place, part == 0),
                 lambda: act(span_copy(0, spans[0], other, part, shards + d)),
             )
             when(target < place, lambda: act(span_copy(1, spans[1], target, part, d)))
+            if part == 0:
+                when(
+                    target < place,
+                    lambda: act(span_copy(1, spans[1], other, part, shards + d)),
+                )
         act(span_copy(0, spans[0], mate, part, 0))
         when(mate < place, lambda: act(span_copy(1, spans[1], mate, part, 0)))
 
@@ -342,7 +352,6 @@
 
     loads["q", 1].wait()
     loop(1, per_span, functools.partial(query_block, 1))
-    pass_on(1)
     wait_halo(1)
     for s in range(2):
         query_block(s, 0)
@@ -354,9 +363,12 @@
         rows = pl.ds(pl.multiple_of(i * block, block), block)
         return pltpu.make_async_copy(out.at[rows, :], low_hbm.at[rows, :], out_sem.at[i])
 
-    def awaited(s, q):
+    def awaited(s, q, part):
+        sent = (q != place) if s == 0 else (q > place)
+        if part == 0:
+            return sent
         passed = jnp.logical_and(lax.rem(q, 2) == lax.rem(place, 2), q > place)
-        return jnp.logical_and(jnp.logical_not(passed), (q != place) if s == 0 else (q > place))
+        return jnp.logical_and(jnp.logical_not(passed), sent)
 
     def needed_parts(index):
         return (block_id(index) * KEEP + part_rows - 1) // part_rows
@@ -367,10 +379,13 @@
         for q in range(shards):
             wanted = jnp.logical_and(q >= low, q < high)
 
-            @pl.when(jnp.logical_and(wanted, awaited(s, q)))
-            def _():
-                for part in range(2):
+            for part in range(2):
+
+                @pl.when(jnp.logical_and(wanted, awaited(s, q, part)))
+                def _():
                     arrive(s, q, part)
+
+    pass_on(1)
 
     handed = [
         pltpu.make_async_copy(source, target, hand_sem.at[n])
@@ -385,7 +400,6 @@
     handed[0].start()
     handed[1].start()
 
-    pass_on(0)
     await_spans(0, 0, lower_spans)
 
     count = 2 - per_span % 2
@@ -401,7 +415,7 @@
 
         most = FAR_PARTS // 2
         attend_blocks(
-            qc, kvc, gath, None, gain, out, index, count, block_id(index), part_rows, 1, most
+            qc, kvc, gath, gain, out, index, count, block_id(index), part_rows, 1, most
         )
         for k in range(count):
             low_copy(index + k).start()
@@ -423,8 +437,8 @@
 
     for part in range(2):
         own_copies(part, lambda copy: copy.wait_send())
-        for d in range(1, chips):
-            passed_copies(part, d, lambda copy: copy.wait_send())
+    for d in range(1, chips):
+        passed_copies(1, d, lambda copy: copy.wait_send())
 
 
 def upper_kernel(
@@ -443,7 +457,6 @@
     gain,
     out,
     low,
-    turned,
     in_sem,
     q_sem,
     out_sem,
@@ -483,7 +496,6 @@
 
     for copy in loads:
         copy.wait()
-    turned[...] = gath[...].reshape(turned.shape[1], -1)[:, :HEAD_CHANNELS].T
 
     count = 2 - per_span % 2
 
@@ -494,7 +506,7 @@
         block_id = block_of(place, shards, per_span, per_span + i)
         least = FAR_PARTS // 2
         attend_blocks(
-            qc, kvc, gath, turned, gain, out, i, count, block_id, part_rows, least, FAR_PARTS
+            qc, kvc, gath, gain, out, i, count, block_id, part_rows, least, FAR_PARTS
         )
         for k in range(count):
             out_copy(i + k).start()
@@ -579,7 +591,6 @@
             pltpu.VMEM((1, columns), f32),
             pltpu.VMEM((span_rows, columns), bf16),
             pltpu.VMEM((span_rows, columns), bf16),
-            pltpu.VMEM((HEAD_CHANNELS, 2 * shards * half), bf16),
             dma((3,)),
             dma((per_span,)),
             dma((per_span,)),

time: 16.7 us -> 15.7 us (0.940)
  Pallas kernels: 16.5 us -> 15.5 us
    pallas_call x1, Pallas kernels: 11.3 us -> 10.4 us  [attention(): pl.pallas_call(functools.partial(kernel, shards, per_span, heads), out_sh...]
where the time goes in v9:
time: 15.7 us; the launch traced here: 15.5 us
  Pallas kernels  15.5 us (99%)
    pallas_call x1, Pallas kernels, attention(): pl.pallas_call(functools.partial(kernel, shards, per_span, heads), out_sh...  10.4 us
    pallas_call x1, Pallas kernels, attention(): pl.pallas_call(functools.partial(upper_kernel, shards, per_span, heads),...  5.12 us

profile of v9, /device:TPU:0, one launch (start us, length us, event | category | flops | bytes accessed | tf_op | source)
XLA Modules:
  0.0 15.5 jit_solution(12464879435112760061)
XLA Ops:
  0.0 10.4 %exchange_and_lower.1 = (bf16[512,512]{1,0:T(8,128)(2,1)}, bf16[4,4,128,128]{3,2,1,0:T(8,128)(2,1)}, bf16[4,128,256]{2,1,0:T(8,128)(2,1)}, bf16[8,64,256]{2,1,0:T(8,128)(2,1)}) custom-call(bf16[1024,512]{1,0:T(8,128)(2,1)} %q_hbm.1, bf16[1024,256]{1,0:T(8,128)(2,1)} %kv_hbm.1, f32[4,512]{1,0:T(4,128)} %qt_hbm.1, f32[4,256]{1,0:T(4,128)} %pt_hbm.1, ...), custom_call_target="tpu_custom_call" | custom-call | tf_op jit(solution)/shard_map/exchange_and_lower/pallas_call | solution.py:539
  10.4 5.1 %upper.1 = bf16[1024,512]{1,0:T(8,128)(2,1)} custom-call(bf16[512,512]{1,0:T(8,128)(2,1)} %get-tuple-element.9.low_hbm, bf16[4,4,128,128]{3,2,1,0:T(8,128)(2,1)} %get-tuple-element.10.qc_hbm, bf16[4,128,256]{2,1,0:T(8,128)(2,1)} %get-tuple-element.11.kvc_hbm, bf16[8,64,256]{2,1,0:T(8,128)(2,1)} %get-tuple-element.12.gath_hbm, f32[1,512]{1,0:T(1,128)} %bitcast.2), custom_call_target="tpu_custom_call" | custom-call | tf_op jit(solution)/shard_map/upper/pallas_call | solution.py:582
